TPU v7x, 128 devices: a whole 4x4x4 slice. The times are simulated.
128 devices in a mesh: enc: 4 (over z), region: 32 (over y, x, core).
Axes of the slice: x: 4, y: 4, z: 4, core: 2. Of those that a mesh axis runs over, the one named last changes fastest.
Arguments:
- embeddings: bfloat16 [131072, 1536], P(('enc', 'region')), may hold values from -6 to 6
- tile_position: int32 [131072], P(('enc', 'region')), may hold values from 0 to 131071, as said below
- w_in: bfloat16 [1536, 768], replicated, may hold values from -0.15625 to 0.15625
- ln_gain: bfloat16 [768], replicated, may hold values from 0.099609375 to 1.8984375
- w_query: bfloat16 [768, 768], replicated, may hold values from -0.14505926 to 0.14505926
- w_key: bfloat16 [768, 768], replicated, may hold values from -1.8222618 to 1.8222618
- w_value: bfloat16 [768, 768], replicated, may hold values from -0.21875 to 0.21875
- w_out: bfloat16 [768, 768], replicated, may hold values from -0.21875 to 0.21875
- near_lengths: int32 [4, 256], replicated, may hold values from 1 to 256, 32768 in all within a row
- far_lengths: int32 [4, 64], replicated, may hold values from 1 to 1024, 32768 in all within a row
- tissue: int32 [131072], P(('enc', 'region')), may hold values 0 or 1
- hospital: int32 [4], replicated, may hold values from 0 to 1, as said below
- w_kernel: float32 [768, 256], replicated, may hold values from -0.21875 to 0.21875
Outputs:
- features: bfloat16 [131072, 768], P(('enc', 'region'))
- statistic: float32 [], replicated
- kernel_grad: float32 [768, 256], replicated
Inputs may be any that keep to these rules, and one draw needn't show every extreme that they name: `tile_position`: every number of 0 to 131071 appears once; the 1024 rows of each device hold exactly 8 positions of each device's block of 1024 consecutive tile positions. `hospital`: each of the two labels is held by at least one of the 4 slides.
All inputs are finite; a program needn't handle non-finite values. No bound on the sum of `tissue` on one device may be relied on, other than what follows from the above.
Results may differ from a plain program's by a relative error of at most 0.012.
Values may be sent and summed in bfloat16 or wider, within the bound.
A program may use at most 128 MiB of HBM per device.

v0:
```python
import jax
import jax.numpy as jnp
from jax import lax
from jax.sharding import PartitionSpec as P

HEADS = 16
REGION = 256
DILATION = 4


NORM_EPSILON = 1e-05
MASKED_SCORE = -1e30
GRAD_SCALE = 100.0


def with_halo(x, sides, width):
    for axis, dim in sides:
        devices, length = (lax.axis_size(axis), x.shape[dim])
        up = [(i, (i + 1) % devices) for i in range(devices - 1)]
        down = [(j, i) for i, j in up]
        last = lax.slice_in_dim(x, length - width, length, axis=dim)
        initial = lax.slice_in_dim(x, 0, width, axis=dim)
        before = lax.ppermute(last, axis, up)
        after = lax.ppermute(initial, axis, down)
        x = jnp.concatenate([before, x, after], axis=dim)
    return x


def layer_norm(inputs):
    center = inputs - jnp.mean(inputs, axis=-1, keepdims=True)
    spread = jnp.mean(center * center, axis=-1, keepdims=True)
    return center * lax.rsqrt(spread + NORM_EPSILON)


def segment_ids(positions, lengths):
    segment_ends = jnp.cumsum(lengths, dtype=jnp.int32)
    passed = (segment_ends <= positions[..., None]).astype(jnp.int32)
    return jnp.sum(passed, axis=-1, dtype=jnp.int32)


def attend(queries, key_rows, values, key_pos, query_seg, key_seg, slide_len):
    scaling = queries.shape[-1] ** (-0.5)
    scores = (
        jnp.einsum("bqhe,bkhe->bhqk", queries, key_rows, preferred_element_type=jnp.float32)
        * scaling
    )
    allowed = (
        (query_seg[:, :, None] == key_seg[:, None, :])
        & (key_pos[:, None, :] >= 0)
        & (key_pos[:, None, :] < slide_len)
    )
    allowed = allowed[:, None, :, :]
    masked = jnp.where(allowed, scores, MASKED_SCORE)
    row_peak = jnp.max(masked, axis=-1, keepdims=True)
    exponent = jnp.where(allowed, jnp.exp(masked - row_peak), 0.0)
    row_total = jnp.sum(exponent, axis=-1, keepdims=True)
    weights = (exponent / row_total).astype(jnp.bfloat16)
    context = jnp.einsum("bhqk,bkhe->bqhe", weights, values, preferred_element_type=jnp.float32)
    return context.astype(jnp.bfloat16)


def block_context(queries, near_kv, far_kv, base_pos, near_row, far_row, slide_len):
    tile_rows, width = queries.shape
    half_width = width // 2
    head_count = HEADS // 2
    head_size = width // HEADS
    near_span = tile_rows // 4
    half_rows = tile_rows // 2
    steps_near = jnp.arange(tile_rows, dtype=jnp.int32)
    near_query = queries[:, :half_width].reshape(2, half_rows, head_count, head_size)
    near_keys = jnp.stack(
        [near_kv[0, :tile_rows], near_kv[0, half_rows : half_rows + tile_rows]]
    ).reshape(2, tile_rows, head_count, head_size)
    near_values = jnp.stack(
        [near_kv[1, :tile_rows], near_kv[1, half_rows : half_rows + tile_rows]]
    ).reshape(2, tile_rows, head_count, head_size)
    query_pos = base_pos + steps_near.reshape(2, half_rows)
    key_pos = base_pos - near_span + jnp.stack([steps_near, steps_near + half_rows])
    near_context = attend(
        near_query,
        near_keys,
        near_values,
        key_pos,
        segment_ids(query_pos, near_row),
        segment_ids(key_pos, near_row),
        slide_len,
    )
    near_context = near_context.reshape(tile_rows, half_width)
    group_rows = tile_rows // DILATION
    far_query = (
        queries[:, half_width:]
        .reshape(group_rows, DILATION, head_count, head_size)
        .transpose(1, 0, 2, 3)
    )
    far_keys = (
        far_kv[0].reshape(3 * group_rows, DILATION, head_count, head_size).transpose(1, 0, 2, 3)
    )
    far_values = (
        far_kv[1].reshape(3 * group_rows, DILATION, head_count, head_size).transpose(1, 0, 2, 3)
    )
    offsets = jnp.arange(DILATION, dtype=jnp.int32)[:, None]
    far_query_pos = base_pos + DILATION * jnp.arange(group_rows, dtype=jnp.int32)[None, :] + offsets
    far_key_pos = (
        base_pos
        - tile_rows
        + DILATION * jnp.arange(3 * group_rows, dtype=jnp.int32)[None, :]
        + offsets
    )
    far_context = attend(
        far_query,
        far_keys,
        far_values,
        far_key_pos,
        segment_ids(far_query_pos, far_row),
        segment_ids(far_key_pos, far_row),
        slide_len,
    )
    far_context = far_context.transpose(1, 0, 2, 3).reshape(tile_rows, half_width)
    return jnp.concatenate([near_context, far_context], axis=1)


def gaussian(left, right):
    left_sq = jnp.sum(left * left, axis=1)
    right_sq = jnp.sum(right * right, axis=1)
    inner = jnp.dot(left, right.T, precision=lax.Precision.HIGHEST)
    return jnp.exp(-(left_sq[:, None] + right_sq[None, :] - 2.0 * inner) / (2.0 * left.shape[1]))


def local(
    embeddings,
    tile_position,
    w_in,
    ln_gain,
    w_query,
    w_key,
    w_value,
    w_out,
    near_lengths,
    far_lengths,
    tissue,
    hospital,
    w_kernel,
):
    tile_rows = embeddings.shape[0]
    enc_count = lax.axis_size("enc")
    region_count = lax.axis_size("region")
    senders = enc_count * region_count
    per_peer = tile_rows // senders
    outgoing = jnp.argsort(tile_position)
    sorted_pos = tile_position[outgoing]
    payload = embeddings[outgoing]
    width_sent = payload.shape[1]
    arrived, arrived_pos = (
        lax.all_to_all(
            payload.reshape(senders, per_peer, width_sent),
            ("enc", "region"),
            split_axis=0,
            concat_axis=0,
            tiled=True,
        ),
        lax.all_to_all(
            sorted_pos.reshape(senders, per_peer),
            ("enc", "region"),
            split_axis=0,
            concat_axis=0,
            tiled=True,
        ),
    )
    placing = jnp.argsort(arrived_pos.reshape(tile_rows) % tile_rows)
    landed = arrived.reshape(tile_rows, width_sent)[placing]
    start_rows = jnp.dot(landed, w_in, preferred_element_type=jnp.float32).astype(jnp.bfloat16)
    normed = (layer_norm(start_rows.astype(jnp.float32)) * ln_gain.astype(jnp.float32)).astype(
        jnp.bfloat16
    )
    queries = jnp.dot(normed, w_query, preferred_element_type=jnp.float32).astype(jnp.bfloat16)
    d_model = queries.shape[1]
    half_width = d_model // 2
    near_span = tile_rows // 4
    base_pos = lax.axis_index("region") * tile_rows
    slide_len = tile_rows * region_count
    near_own = jnp.einsum(
        "rd,sdc->src",
        normed,
        jnp.stack([w_key[:, :half_width], w_value[:, :half_width]]),
        preferred_element_type=jnp.float32,
    ).astype(jnp.bfloat16)
    far_own = jnp.einsum(
        "rd,sdc->src",
        normed,
        jnp.stack([w_key[:, half_width:], w_value[:, half_width:]]),
        preferred_element_type=jnp.float32,
    ).astype(jnp.bfloat16)
    near_kv = with_halo(near_own, (("region", 1),), near_span)
    far_kv = with_halo(far_own, (("region", 1),), tile_rows)
    slide_index = lax.axis_index("enc")
    near_row = lax.dynamic_index_in_dim(near_lengths, slide_index, 0, keepdims=False)
    far_row = lax.dynamic_index_in_dim(far_lengths, slide_index, 0, keepdims=False)
    context = block_context(queries, near_kv, far_kv, base_pos, near_row, far_row, slide_len)
    features = (
        start_rows.astype(jnp.float32) + jnp.dot(context, w_out, preferred_element_type=jnp.float32)
    ).astype(jnp.bfloat16)
    reg_dev = tile_rows // REGION
    per_slide = reg_dev * region_count
    region_total = reg_dev * senders
    pooled = (
        jnp.einsum(
            "grd,gr->gd",
            features.reshape(reg_dev, REGION, d_model),
            tissue.reshape(reg_dev, REGION).astype(jnp.bfloat16),
            preferred_element_type=jnp.float32,
        )
        / REGION
    )
    normal_pool = layer_norm(pooled)
    slide_ids = jnp.arange(hospital.shape[0], dtype=jnp.int32)
    labelled_one = jnp.sum(hospital).astype(jnp.float32)
    count_one = labelled_one * per_slide
    count_zero = (hospital.shape[0] - labelled_one) * per_slide

    def region_weights(region_ids):
        owner_slide = region_ids // per_slide
        label_of = jnp.sum(
            jnp.where(owner_slide[:, None] == slide_ids[None, :], hospital[None, :], 0), axis=1
        )
        return jnp.where(label_of == 1, 1.0 / count_one, -1.0 / count_zero)

    embedded = jnp.dot(normal_pool, w_kernel, precision=lax.Precision.HIGHEST)
    device_pos = lax.axis_index("enc") * region_count + lax.axis_index("region")
    own_weights = region_weights(device_pos * reg_dev + jnp.arange(reg_dev, dtype=jnp.int32))
    piece = lax.all_gather(embedded, ("enc", "region"), axis=0, tiled=True)
    piece_ids = jnp.arange(piece.shape[0], dtype=jnp.int32)
    weighted = gaussian(embedded, piece) * region_weights(piece_ids)[None, :]
    kernel_sums = jnp.sum(weighted, axis=1)
    moments = jnp.dot(weighted, piece, precision=lax.Precision.HIGHEST)
    stat_part = region_total * jnp.sum(own_weights * kernel_sums)
    grad_embedded = (
        -2.0
        * region_total
        / embedded.shape[1]
        * own_weights[:, None]
        * (kernel_sums[:, None] * embedded - moments)
    )
    grad_part = GRAD_SCALE * jnp.dot(normal_pool.T, grad_embedded, precision=lax.Precision.HIGHEST)
    statistic, kernel_grad = lax.psum((stat_part, grad_part), ("enc", "region"))
    return (features, statistic, kernel_grad)


def solution(mesh):
    return jax.shard_map(
        local,
        mesh=mesh,
        in_specs=(
            P(("enc", "region"), None),
            P(("enc", "region")),
            P(),
            P(),
            P(),
            P(),
            P(),
            P(),
            P(),
            P(),
            P(("enc", "region")),
            P(),
            P(),
        ),
        out_specs=(P(("enc", "region"), None), P(), P()),
        check_vma=False,
    )
```

profile of v0, /device:TPU:1, one launch (start us, length us, event | category | flops | bytes accessed | tf_op | source)
XLA Modules:
  0.0 473.4 jit_solution(16803794036345877216)
XLA Ops:
  7.2 5.2 %sort.31 = (s32[1024]{0:T(1024)}, s32[1024]{0:T(1024)S(1)}) sort(s32[1024]{0:T(1024)} %param.14, s32[1024]{0:T(1024)S(1)} %iota.81), dimensions={0}, to_apply=%region_0.0 | sort | flops 10240 | bytes 16384 | tf_op jit(solution)/shard_map/jit(argsort)/sort | solution.py:149
  12.4 5.7 %gather_fusion.1 = s32[1024]{0:T(1024)S(1)} fusion(s32[1024]{0:T(1024)} %param.14, s32[1024]{0:T(1024)S(1)} %fusion.90), kind=kCustom, calls=%fused_computation.1 | custom fusion | bytes 12288 | tf_op jit(solution)/shard_map/gather | solution.py:150
  18.9 11.5 %all-to-all-start.1 = ((s32[128,1,8]{2,1,0:T(1,128)}), s32[128,1,8]{2,1,0:T(1,128)S(1)}, u32[]{:S(2)}, u32[]{:S(2)}) async-start(s32[128,1,8]{2,1,0:T(1,128)} %bitcast.2), calls=%async_computation.1 | async-start | bytes 131072 | tf_op jit(solution)/shard_map/all_to_all | solution.py:161
  30.4 2.5 fusion.111
  37.4 5.6 %gather_fusion = bf16[1024,1536]{1,0:T(8,128)(2,1)} fusion(bf16[1024,1536]{1,0:T(8,128)(2,1)S(1)} %copy-done, s32[1024]{0:T(1024)S(1)} %fusion.90), kind=kCustom, calls=%fused_computation | custom fusion | bytes 6295552 | tf_op jit(solution)/shard_map/gather | solution.py:151
  52.1 9.8 %all-to-all-start = ((bf16[128,8,1536]{2,1,0:T(8,128)(2,1)}), bf16[128,8,1536]{2,1,0:T(8,128)(2,1)S(1)}, u32[]{:S(2)}, u32[]{:S(2)}) async-start(bf16[128,8,1536]{2,1,0:T(8,128)(2,1)} %bitcast.105), calls=%async_computation | async-start | bytes 6291456 | tf_op jit(solution)/shard_map/all_to_all | solution.py:154
  69.5 4.4 sort.32
  73.9 29.5 %all-to-all-done = bf16[128,8,1536]{2,1,0:T(8,128)(2,1)S(1)} async-done(((bf16[128,8,1536]{2,1,0:T(8,128)(2,1)}), bf16[128,8,1536]{2,1,0:T(8,128)(2,1)S(1)}, u32[]{:S(2)}, u32[]{:S(2)}) %all-to-all-start) | async-done | bytes 3145760 | tf_op jit(solution)/shard_map/all_to_all | solution.py:154
  103.4 5.6 %gather_fusion.2 = bf16[1024,1536]{1,0:T(8,128)(2,1)} fusion(bf16[1024,1536]{1,0:T(8,128)(2,1)S(1)} %bitcast.104, s32[1024]{0:T(1024)S(1)} %fusion.91), kind=kCustom, calls=%fused_computation.2 | custom fusion | bytes 6295552 | tf_op jit(solution)/shard_map/gather | solution.py:170
  109.0 5.4 %convert_reduce_fusion = (f32[1024]{0:T(1024)S(1)}, bf16[1024,768]{1,0:T(8,128)(2,1)S(1)}) fusion(bf16[1024,1536]{1,0:T(8,128)(2,1)} %gather_fusion.2, bf16[1536,768]{1,0:T(8,128)(2,1)} %param.15), kind=kOutput, calls=%fused_computation.24 | convolution fusion | flops 2418277376 | bytes 7081984 | tf_op jit(solution)/shard_map/dot_general | solution.py:171
  115.1 2.7 fusion.46
  117.8 3.1 collective-permute-start.3
  120.9 2.5 collective-permute-start.2
  125.9 3.0 collective-permute-start.1
  128.9 2.7 collective-permute-start
  134.3 3.1 reshape.336
  147.6 22.4 %fusion.121 = (f32[2,8,512]{2,1,0:T(8,128)S(1)}, f32[2,8,512,1024]{3,2,1,0:T(8,128)}) fusion(bf16[2,1024,8,48]{1,3,2,0:T(8,128)(2,1)} %bitcast.109, pred[2,512,1024]{2,1,0:T(8,128)(4,1)} %and_and_fusion, bf16[2,512,8,48]{1,0,3,2:T(2,128)(2,1)} %reshape.331), kind=kOutput, calls=%fused_computation.160 | convolution fusion | flops 847250432 | bytes 36995072 | tf_op jit(solution)/shard_map/sub | solution.py:55
  169.9 13.5 %fusion.56 = bf16[2,512,8,48]{1,3,2,0:T(8,128)(2,1)S(1)} fusion(bf16[2,1024,8,48]{1,3,2,0:T(8,128)(2,1)S(1)} %bitcast.108, f32[2,8,512,1024]{3,2,1,0:T(8,128)} %get-tuple-element.30, f32[2,8,512]{2,1,0:T(8,128)S(1)} %get-tuple-element.29), kind=kOutput, calls=%fused_computation.67 | convolution fusion | flops 822476800 | bytes 35946496 | tf_op jit(solution)/shard_map/bhqk,bkhe->bqhe/dot_general | solution.py:58
  185.3 2.5 pad_maximum_fusion
  189.5 4.3 copy.68
  193.8 9.3 %reshape_squeeze.7 = bf16[768,4,8,48]{3,2,1,0:T(8,128)(2,1)} reshape(bf16[1,3072,384]{2,1,0:T(8,128)(2,1)} %copy.68) | data formatting | bytes 4718592 | tf_op jit(solution)/shard_map/reshape;squeeze | solution.py:96
  203.1 7.9 %copy.69 = bf16[768,4,8,48]{0,3,2,1:T(8,128)(2,1)} copy(bf16[768,4,8,48]{3,2,1,0:T(8,128)(2,1)} %reshape_squeeze.7) | data formatting | bytes 4718592 | tf_op jit(solution)/shard_map/reshape;squeeze | solution.py:96
  211.0 2.6 copy.64
  213.6 9.3 %reshape_squeeze.6 = bf16[768,4,8,48]{3,2,1,0:T(8,128)(2,1)} reshape(bf16[1,3072,384]{2,1,0:T(8,128)(2,1)} %copy.64) | data formatting | bytes 4718592 | tf_op jit(solution)/shard_map/reshape;squeeze | solution.py:99
  222.9 8.1 %copy.65 = bf16[768,4,8,48]{0,3,2,1:T(8,128)(2,1)} copy(bf16[768,4,8,48]{3,2,1,0:T(8,128)(2,1)} %reshape_squeeze.6) | data formatting | bytes 4718592 | tf_op jit(solution)/shard_map/reshape;squeeze | solution.py:99
  230.9 16.9 %fusion.112 = (f32[4,8,256]{2,1,0:T(8,128)S(1)}, f32[4,8,256,768]{3,2,1,0:T(8,128)}) fusion(pred[4,256,768]{2,1,0:T(8,128)(4,1)S(1)} %copy-done.9, bf16[768,4,8,48]{0,3,2,1:T(8,128)(2,1)S(1)} %copy-done.5, bf16[256,4,8,48]{0,3,2,1:T(8,128)(2,1)} %copy.67), kind=kOutput, calls=%fused_computation.159 | convolution fusion | flops 635437824 | bytes 29130752 | tf_op jit(solution)/shard_map/sub | solution.py:55
  247.9 11.4 %fusion.53 = bf16[256,4,8,48]{0,3,2,1:T(8,128)(2,1)S(1)} fusion(f32[4,8,256,768]{3,2,1,0:T(8,128)} %get-tuple-element.28, f32[4,8,256]{2,1,0:T(8,128)S(1)} %get-tuple-element.27, bf16[768,4,8,48]{0,3,2,1:T(8,128)(2,1)} %copy.65), kind=kOutput, calls=%fused_computation.65 | convolution fusion | flops 616955904 | bytes 28344320 | tf_op jit(solution)/shard_map/bhqk,bkhe->bqhe/dot_general | solution.py:58
  259.3 3.0 copy.70
  264.9 3.7 fusion.19
  271.1 40.2 %all-gather = f32[128,4,256]{2,1,0:T(4,128)} all-gather(f32[1,4,256]{2,1,0:T(4,128)S(1)} %bitcast.115), channel_id=1, replica_groups=mesh['enc'=4,'region'=32] {'enc','region'}, dimensions={0}, use_global_device_ids=true | all-gather | bytes 528384 | tf_op jit(solution)/shard_map/all_gather | solution.py:230
  320.6 64.7 %psum.14 = f32[]{:T(128)} all-reduce(f32[]{:T(128)S(6)} %mul.163), channel_id=1, replica_groups=mesh['enc'=4,'region'=32] {'enc','region'}, use_global_device_ids=true, to_apply=%region_24.25 | all-reduce | flops 1 | bytes 8 | tf_op jit(solution)/shard_map/psum | solution.py:244
  385.4 78.6 %all-reduce.2.cloned.1.call-done = f32[768,256]{1,0:T(8,128)} async-done(((f32[768,256]{1,0:T(8,128)}), f32[768,256]{1,0:T(8,128)}) %all-reduce.2.cloned.1.call-update) | async-done | bytes 786448 | tf_op jit(solution)/shard_map/psum | solution.py:244
  (129 shorter events, 56.4 us)
Async XLA Ops:
  7.2 30.2 %copy-start = (bf16[1024,1536]{1,0:T(8,128)(2,1)S(1)}, bf16[1024,1536]{1,0:T(8,128)(2,1)}, u32[]{:S(2)}) copy-start(bf16[1024,1536]{1,0:T(8,128)(2,1)} %param.13) | copy-start | bytes 9437188
  18.1 17.2 %copy-start.19 = (s32[4]{0:T(128)S(1)}, s32[4]{0:T(128)}, u32[]{:S(2)}) copy-start(s32[4]{0:T(128)} %param.24) | copy-start | bytes 52
  18.9 33.2 %all-to-all-start.1 = ((s32[128,1,8]{2,1,0:T(1,128)}), s32[128,1,8]{2,1,0:T(1,128)S(1)}, u32[]{:S(2)}, u32[]{:S(2)}) async-start(s32[128,1,8]{2,1,0:T(1,128)} %bitcast.2), calls=%async_computation.1 | async-start | bytes 131072 | tf_op jit(solution)/shard_map/all_to_all | solution.py:161
  30.4 2.5 copy-start.8
  37.4 10.1 %copy-start.18 = (bf16[768]{0:T(1024)(128)(2,1)S(1)}, bf16[768]{0:T(1024)(128)(2,1)}, u32[]{:S(2)}) copy-start(bf16[768]{0:T(1024)(128)(2,1)} %param.16) | copy-start | bytes 4612
  43.0 6.7 %copy-start.4 = (bf16[768,384]{1,0:T(8,128)(2,1)S(1)}, bf16[768,384]{1,0:T(8,128)(2,1)}, u32[]{:S(2)}) copy-start(bf16[768,384]{1,0:T(8,128)(2,1)} %get-tuple-element.17) | copy-start | bytes 1769476
  43.0 8.4 %copy-start.17 = (s32[1024]{0:T(1024)S(1)}, s32[1024]{0:T(1024)}, u32[]{:S(2)}) copy-start(s32[1024]{0:T(1024)} %param.23) | copy-start | bytes 12292
  52.1 51.3 %all-to-all-start = ((bf16[128,8,1536]{2,1,0:T(8,128)(2,1)}), bf16[128,8,1536]{2,1,0:T(8,128)(2,1)S(1)}, u32[]{:S(2)}, u32[]{:S(2)}) async-start(bf16[128,8,1536]{2,1,0:T(8,128)(2,1)} %bitcast.105), calls=%async_computation | async-start | bytes 6291456 | tf_op jit(solution)/shard_map/all_to_all | solution.py:154
  61.9 402.1 %all-reduce.2.cloned.1.call-start = ((), (), s32[]{:S(2)}) async-start(), calls=%async_computation.2 | async-start | bytes 1572864 | tf_op jit(solution)/shard_map/psum | solution.py:244
  109.0 6.0 %copy-start.13 = (bf16[768,384]{0,1:T(8,128)(2,1)S(1)}, bf16[768,384]{0,1:T(8,128)(2,1)}, u32[]{:S(2)}) copy-start(bf16[768,384]{0,1:T(8,128)(2,1)} %copy.77) | copy-start | bytes 1769476
  109.0 6.0 %copy-start.14 = (bf16[768,384]{0,1:T(8,128)(2,1)S(1)}, bf16[768,384]{0,1:T(8,128)(2,1)}, u32[]{:S(2)}) copy-start(bf16[768,384]{0,1:T(8,128)(2,1)} %copy.76) | copy-start | bytes 1769476
  114.4 17.2 %copy-start.6 = (bf16[1024,768]{1,0:T(8,128)(2,1)}, bf16[1024,768]{1,0:T(8,128)(2,1)S(1)}, u32[]{:S(2)}) copy-start(bf16[1024,768]{1,0:T(8,128)(2,1)S(1)} %get-tuple-element.26) | copy-start | bytes 4718596
  115.0 8.3 %copy-start.11 = (bf16[768,384]{0,1:T(8,128)(2,1)S(1)}, bf16[768,384]{0,1:T(8,128)(2,1)}, u32[]{:S(2)}) copy-start(bf16[768,384]{0,1:T(8,128)(2,1)} %copy.75) | copy-start | bytes 1769476
  115.1 8.3 %copy-start.12 = (bf16[768,384]{0,1:T(8,128)(2,1)S(1)}, bf16[768,384]{0,1:T(8,128)(2,1)}, u32[]{:S(2)}) copy-start(bf16[768,384]{0,1:T(8,128)(2,1)} %copy.74) | copy-start | bytes 1769476
  117.8 67.5 %collective-permute-start.3 = (bf16[2,1024,384]{1,2,0:T(8,128)(2,1)}, bf16[2,1024,384]{1,2,0:T(8,128)(2,1)}, u32[]{:S(2)}, u32[]{:S(2)}) collective-permute-start(bf16[2,1024,384]{1,2,0:T(8,128)(2,1)} %fusion.46), channel_id=1, source_target_pairs={{1,0},{2,1},{3,2},{4,3},{5,4},{6,5},{7,6},{8,7},{9,8},{10,9},{11,1... | collective-permute-start | bytes 4718600 | tf_op jit(solution)/shard_map/ppermute | solution.py:24
  120.9 64.4 %collective-permute-start.2 = (bf16[2,1024,384]{1,2,0:T(8,128)(2,1)}, bf16[2,1024,384]{1,2,0:T(8,128)(2,1)}, u32[]{:S(2)}, u32[]{:S(2)}) collective-permute-start(bf16[2,1024,384]{1,2,0:T(8,128)(2,1)} %fusion.46), channel_id=1, source_target_pairs={{0,1},{1,2},{2,3},{3,4},{4,5},{5,6},{6,7},{7,8},{8,9},{9,10},{10,1... | collective-permute-start | bytes 4718600 | tf_op jit(solution)/shard_map/ppermute | solution.py:23
  123.4 8.3 %copy-start.21 = (bf16[768,768]{1,0:T(8,128)(2,1)S(1)}, bf16[768,768]{1,0:T(8,128)(2,1)}, u32[]{:S(2)}) copy-start(bf16[768,768]{1,0:T(8,128)(2,1)} %param.17) | copy-start | bytes 3538948
  125.0 8.2 %copy-start.2 = (bf16[2,1024,384]{1,2,0:T(8,128)(2,1)}, bf16[2,1024,384]{1,2,0:T(8,128)(2,1)S(1)}, u32[]{:S(2)}) copy-start(bf16[2,1024,384]{1,2,0:T(8,128)(2,1)S(1)} %fusion.43) | copy-start | bytes 4718596
  125.9 18.2 %collective-permute-start.1 = (bf16[2,256,384]{1,2,0:T(8,128)(2,1)}, bf16[2,256,384]{1,2,0:T(8,128)(2,1)}, u32[]{:S(2)}, u32[]{:S(2)}) collective-permute-start(bf16[2,256,384]{1,2,0:T(8,128)(2,1)} %get-tuple-element.16), channel_id=1, source_target_pairs={{1,0},{2,1},{3,2},{4,3},{5,4},{6,5},{7,6},{8,7},{9,8},{10,9},{11,1... | collective-permute-start | bytes 1179656 | tf_op jit(solution)/shard_map/ppermute | solution.py:24
  128.9 16.2 %collective-permute-start = (bf16[2,256,384]{1,2,0:T(8,128)(2,1)S(1)}, bf16[2,256,384]{1,2,0:T(8,128)(2,1)}, u32[]{:S(2)}, u32[]{:S(2)}) collective-permute-start(bf16[2,256,384]{1,2,0:T(8,128)(2,1)S(1)} %get-tuple-element.15), channel_id=1, source_target_pairs={{0,1},{1,2},{2,3},{3,4},{4,5},{5,6},{6,7},{7,8},{8,9},{9,10},{10,1... | collective-permute-start | bytes 1179656 | tf_op jit(solution)/shard_map/ppermute | solution.py:23
  139.8 5.3 %copy-start.3 = (bf16[2,1024,384]{1,2,0:T(8,128)(2,1)S(1)}, bf16[2,1024,384]{1,2,0:T(8,128)(2,1)}, u32[]{:S(2)}) copy-start(bf16[2,1024,384]{1,2,0:T(8,128)(2,1)} %copy-done.2) | copy-start | bytes 4718596
  222.8 8.1 %copy-start.5 = (bf16[768,4,8,48]{0,3,2,1:T(8,128)(2,1)S(1)}, bf16[768,4,8,48]{0,3,2,1:T(8,128)(2,1)}, u32[]{:S(2)}) copy-start(bf16[768,4,8,48]{0,3,2,1:T(8,128)(2,1)} %copy.69) | copy-start | bytes 7077892
  222.9 8.1 %copy-start.9 = (pred[4,256,768]{2,1,0:T(8,128)(4,1)S(1)}, pred[4,256,768]{2,1,0:T(8,128)(4,1)}, u32[]{:S(2)}) copy-start(pred[4,256,768]{2,1,0:T(8,128)(4,1)} %and_and_fusion.1) | copy-start | bytes 2359300
  264.9 4.9 %copy-start.15 = (bf16[4,256,1]{1,2,0:T(2,128)(2,1)S(1)}, bf16[4,256,1]{1,2,0:T(2,128)(2,1)}, u32[]{:S(2)}) copy-start(bf16[4,256,1]{1,2,0:T(2,128)(2,1)} %reshape.372) | copy-start | bytes 6148
  264.9 5.5 %copy-start.10 = (f32[768,256]{1,0:T(8,128)S(1)}, f32[768,256]{1,0:T(8,128)}, u32[]{:S(2)}) copy-start(f32[768,256]{1,0:T(8,128)} %param.25) | copy-start | bytes 2359300
  268.7 1.1 copy-start.7
  268.7 45.8 %copy-start.16 = (f32[512]{0:T(512)S(1)}, f32[512]{0:T(512)}, u32[]{:S(2)}) copy-start(f32[512]{0:T(512)} %compare_select_fusion.2) | copy-start | bytes 6148
  268.7 47.5 %copy-start.20 = (s32[4]{0:T(128)S(1)}, s32[4]{0:T(128)}, u32[]{:S(2)}) copy-start(s32[4]{0:T(128)} %select_reduce_fusion.1) | copy-start | bytes 52
  271.1 195.0 %copy-start.1 = (bf16[1024,1536]{1,0:T(8,128)(2,1)S(1)}, bf16[1024,1536]{1,0:T(8,128)(2,1)}, u32[]{:S(2)}) copy-start(bf16[1024,1536]{1,0:T(8,128)(2,1)} %param.13) | copy-start | bytes 9437188
Sparse Core Ops, SparseCore 0:
  320.1 143.8 all-reduce.1
where the time goes:
time: 479 us; the launch traced here: 473 us
  waiting for transfers between devices  112 us (23%)
  blocking collectives  105 us (22%)
  local copies, waits for them, and re-layouts  96.9 us (20%)
  matrix products  84.8 us (18%)
  starting transfers between devices  33.1 us (7%)
  other arithmetic  25.6 us (5%)
  between operations  16.5 us (3%)
    psum x1, waiting for transfers between devices, local(): statistic, kernel_grad = lax.psum((stat_part, grad_part), ('enc', 'region'))  78.6 us
    psum x1, blocking collectives, local(): statistic, kernel_grad = lax.psum((stat_part, grad_part), ('enc', 'region'))  64.7 us
    all_gather x1, blocking collectives, local(): piece = lax.all_gather(embedded, ('enc', 'region'), axis=0, tiled=True)  40.2 us
    sub x2, matrix products, attend(): exponent = jnp.where(allowed, jnp.exp(masked - row_peak), 0.0)  39.3 us
    all_to_all x1, waiting for transfers between devices, local(): lax.all_to_all(payload.reshape(senders, per_peer, width_sent), ('enc', 'r...  29.5 us
    dot_general x2, matrix products, attend(): jnp.einsum('bhqk,bkhe->bqhe', weights, values, preferred_element_type=jnp...  24.8 us
    another operation x2, local copies, waits for them, and re-layouts, block_context(): far_kv[1].reshape(3 * group_rows, DILATION, head_count, head_size)  17.4 us
    another operation x2, local copies, waits for them, and re-layouts, block_context(): far_kv[0].reshape(3 * group_rows, DILATION, head_count, head_size)  17.2 us
  transfers between devices with their start and end apart: 7, of which 4 were waited for; matrix products, arithmetic and copies ran while one was open for 18% of the time, Pallas kernels for 0%

commit v1 on v0

v1 whole, which is shorter than its diff:
```python
import functools

import jax
import jax.numpy as jnp
from jax import lax
from jax.experimental import pallas as pl
from jax.experimental.pallas import tpu as pltpu
from jax.sharding import PartitionSpec as P

MESH = pl.DeviceIdType.MESH
F32 = jnp.float32
BF16 = jnp.bfloat16
I32 = jnp.int32

ROWS = 1024
DIN = 1536
D = 768
PAIRS = 8
HEAD = 48
LANES = 128
PW = PAIRS // 2 * LANES
GROUP = 256
DIL = 4
REGION = 256
NENC = 4
NREGION = 32
PEERS = NENC * NREGION
CAP = 8
HALF = D // 2
EPS = 1e-05
BIG = 1e30
BITS = 9
PAD_SEG = 511
EXP_SCALE = 1.4426950408889634 / 48.0**0.5
VMEM_LIMIT = 56 * 1024 * 1024


def iota(shape, dim):
    return lax.broadcasted_iota(I32, shape, dim)


def dot(a, b):
    return jnp.dot(a, b, preferred_element_type=F32)


def params(**kw):
    return pltpu.CompilerParams(vmem_limit_bytes=VMEM_LIMIT, **kw)


VM = pl.BlockSpec(memory_space=pltpu.VMEM)


def project_kernel(emb_ref, pos_ref, w_ref, xs_ref, ps_ref, s_ref):
    pos = pos_ref[...].astype(F32)
    eye = iota((LANES, LANES), 0) == iota((LANES, LANES), 1)
    rank = jnp.zeros((1, ROWS), F32)
    for k in range(ROWS // LANES):
        part = pos[:, k * LANES : (k + 1) * LANES]
        col = jnp.sum(jnp.where(eye, part, 0.0), axis=1, keepdims=True)
        rank = rank + jnp.sum(jnp.where(col < pos, 1.0, 0.0), axis=0, keepdims=True)
    rank = rank.astype(I32)
    local = pos_ref[...] % ROWS
    slot = ((local % DIL) * GROUP + local // DIL).astype(F32)
    dest = iota((PEERS, ROWS), 0) * CAP
    lane = iota((PEERS, LANES), 1)
    table = jnp.zeros((PEERS, LANES), F32)
    for c in range(CAP):
        hit = jnp.where(dest + c == rank, slot, 0.0)
        table = jnp.where(lane == c, jnp.sum(hit, axis=1, keepdims=True), table)
    for d in range(PEERS):
        ps_ref[d] = table[d : d + 1, :]
    step = 256
    for k in range(ROWS // step):
        s_ref[pl.ds(k * step, step), :] = dot(
            emb_ref[pl.ds(k * step, step), :], w_ref[...]
        ).astype(BF16)
    for k in range(ROWS // step):
        pick = jnp.where(iota((step, ROWS), 0) + k * step == rank, 1.0, 0.0).astype(BF16)
        moved = dot(pick, s_ref[...]).reshape(step // CAP, CAP, D)
        both = jnp.concatenate([moved[:, :, :HALF], moved[:, :, HALF:]], axis=1)
        xs_ref[pl.ds(k * 2 * step, 2 * step), :] = both.reshape(2 * step, HALF).astype(BF16)


def exchange_kernel(xs_ref, ps_ref, xr_ref, pr_ref, sx, rx, sp, rp, own):
    me = lax.axis_index("enc") * NREGION + lax.axis_index("region")
    chunk = 2 * CAP
    barrier = pltpu.get_barrier_semaphore()

    def signal(k, carry):
        peer = (me + k) % PEERS
        pl.semaphore_signal(
            barrier, inc=1, device_id=(peer // NREGION, peer % NREGION), device_id_type=MESH
        )
        return carry

    lax.fori_loop(1, PEERS, signal, 0)
    mine_x = pltpu.make_async_copy(
        xs_ref.at[pl.ds(me * chunk, chunk), :], xr_ref.at[pl.ds(me * chunk, chunk), :], own.at[0]
    )
    mine_p = pltpu.make_async_copy(ps_ref.at[me], pr_ref.at[me], own.at[1])
    mine_x.start()
    mine_p.start()
    pl.semaphore_wait(barrier, PEERS - 1)

    def send(k, carry):
        peer = (me + k) % PEERS
        where = (peer // NREGION, peer % NREGION)
        pltpu.make_async_remote_copy(
            src_ref=ps_ref.at[peer], dst_ref=pr_ref.at[me],
            send_sem=sp, recv_sem=rp, device_id=where, device_id_type=MESH,
        ).start()
        pltpu.make_async_remote_copy(
            src_ref=xs_ref.at[pl.ds(peer * chunk, chunk), :],
            dst_ref=xr_ref.at[pl.ds(me * chunk, chunk), :],
            send_sem=sx, recv_sem=rx, device_id=where, device_id_type=MESH,
        ).start()
        return carry

    lax.fori_loop(1, PEERS, send, 0)
    mine_x.wait()
    mine_p.wait()
    rest_x = pl.ds(0, (PEERS - 1) * chunk)
    rest_p = pl.ds(0, PEERS - 1)
    pltpu.make_async_copy(ps_ref.at[rest_p], pr_ref.at[rest_p], rp).wait()
    pltpu.make_async_copy(ps_ref.at[rest_p], pr_ref.at[rest_p], sp).wait()
    pltpu.make_async_copy(xs_ref.at[rest_x, :], xr_ref.at[rest_x, :], rx).wait()
    pltpu.make_async_copy(xs_ref.at[rest_x, :], xr_ref.at[rest_x, :], sx).wait()


def land_kernel(xr_ref, pr_ref, gain_ref, start_ref, normed_ref, x_ref):
    table = jnp.concatenate([pr_ref[d] for d in range(PEERS)], axis=0)
    high = jnp.floor(table * (1.0 / 32.0))
    low = table - 32.0 * high
    spread = jnp.where(
        iota((LANES, ROWS), 0) == iota((LANES, ROWS), 1) % CAP, 1.0, 0.0
    ).astype(BF16)
    wide = 32.0 * dot(high.astype(BF16), spread) + dot(low.astype(BF16), spread)
    mine = iota((PEERS, ROWS), 0) == iota((PEERS, ROWS), 1) // CAP
    slot = jnp.sum(jnp.where(mine, wide, 0.0), axis=0, keepdims=True).astype(I32)
    step = 256
    for k in range(ROWS // step):
        got = xr_ref[pl.ds(k * 2 * step, 2 * step), :].astype(F32)
        got = got.reshape(step // CAP, 2 * CAP, HALF)
        both = jnp.concatenate([got[:, :CAP, :], got[:, CAP:, :]], axis=2)
        x_ref[pl.ds(k * step, step), :] = both.reshape(step, D).astype(BF16)
    gain = gain_ref[...].astype(F32)
    for k in range(ROWS // step):
        pick = jnp.where(iota((step, ROWS), 0) + k * step == slot, 1.0, 0.0).astype(BF16)
        rows = dot(pick, x_ref[...])
        start_ref[pl.ds(k * step, step), :] = rows.astype(BF16)
        center = rows - jnp.mean(rows, axis=1, keepdims=True)
        var = jnp.mean(center * center, axis=1, keepdims=True)
        normed_ref[pl.ds(k * step, step), :] = (center * lax.rsqrt(var + EPS) * gain).astype(BF16)


def ends_of(lengths):
    n = lengths.shape[1]
    upto = jnp.where(iota((n, n), 0) <= iota((n, n), 1), 1.0, 0.0).astype(BF16)
    high, low = lengths // 32, lengths % 32
    sums = 32.0 * dot(high.astype(F32).astype(BF16), upto) + dot(low.astype(F32).astype(BF16), upto)
    own = iota(sums.shape, 0) == lax.axis_index("enc")
    return jnp.sum(jnp.where(own, sums, 0.0), axis=0, keepdims=True)


def segment_of(pos, ends):
    seg = jnp.sum(jnp.where(ends <= pos.astype(F32), 1.0, 0.0), axis=1, keepdims=True).astype(I32)
    return jnp.where((pos >= 0) & (pos < ROWS * NREGION), seg, PAD_SEG)


def key_marks(seg):
    lane = iota((seg.shape[0], LANES), 1) - 2 * HEAD
    bit = (seg >> jnp.where(lane >= BITS, lane - BITS, jnp.maximum(lane, 0)) % 16) & 1
    mark = jnp.where(lane < BITS, 1 - bit, bit)
    return jnp.where((lane >= 0) & (lane < 2 * BITS), mark, 0).astype(F32)


def query_marks(seg):
    lane = iota((seg.shape[0], LANES), 1) - 2 * HEAD
    bit = (seg >> jnp.where(lane >= BITS, lane - BITS, jnp.maximum(lane, 0)) % 16) & 1
    mark = jnp.where(lane < BITS, bit, 1 - bit)
    return jnp.where((lane >= 0) & (lane < 2 * BITS), mark, 0).astype(F32) * -BIG


def attend(queries, marks, keys, values):
    n = queries.shape[0]
    lane = iota((n, LANES), 1)
    out = []
    for j in range(PAIRS // 2):
        cols = slice(j * LANES, (j + 1) * LANES)
        both = queries[:, cols]
        kk, vv = keys[:, cols], values[:, cols]
        parts = []
        for h in range(2):
            q = jnp.where((lane >= h * HEAD) & (lane < (h + 1) * HEAD), both, marks)
            s = lax.dot_general(q, kk, (((1,), (1,)), ((), ())), preferred_element_type=F32)
            peak = jnp.max(s, axis=1, keepdims=True)
            p = jnp.exp2((s - peak) * EXP_SCALE).astype(BF16)
            o = dot(p, vv)
            parts.append(o / o[:, 2 * HEAD : 2 * HEAD + 1])
        res = jnp.where(lane < HEAD, parts[0], jnp.where(lane < 2 * HEAD, parts[1], 0.0))
        out.append(res.astype(BF16))
    return jnp.concatenate(out, axis=1)


def layer_kernel(
    start_ref, own_ref, left_ref, right_ref, wq_ref, wk_ref, wv_ref, wo_ref,
    near_ref, far_ref, tissue_ref, feat_ref, pool_ref,
    q_ref, qm_ref, kn_ref, vn_ref, kf_ref, vf_ref, ctx_ref, nat_ref,
):
    base = lax.axis_index("region") * ROWS
    near_ends = ends_of(near_ref[...])
    far_ends = ends_of(far_ref[...])
    near_cols, far_cols = pl.ds(0, PW), pl.ds(PW, PW)
    ones_lane = jnp.where(iota((GROUP, PW), 1) % LANES == 2 * HEAD, 1.0, 0.0)

    def tiled(marks):
        return jnp.concatenate([marks] * (PAIRS // 2), axis=1)

    edge = GROUP // 4
    for o in range(DIL):
        rows = pl.ds(o * GROUP, GROUP)
        for b, ref in enumerate((left_ref, own_ref, right_ref)):
            x = ref[rows, :]
            pos = base + (b - 1) * ROWS + DIL * iota((GROUP, 1), 0) + o
            seg = segment_of(pos, far_ends)
            dst = pl.ds(b * GROUP, GROUP)
            kf_ref[o, dst, :] = (dot(x, wk_ref[:, far_cols]) + tiled(key_marks(seg))).astype(BF16)
            vf_ref[o, dst, :] = (dot(x, wv_ref[:, far_cols]) + ones_lane).astype(BF16)
            if b == 1:
                q_ref[rows, :] = dot(x, wq_ref[...]).astype(BF16)
                qm_ref[1, rows, :] = query_marks(seg).astype(BF16)
            first, count = ((GROUP - edge, edge), (0, GROUP), (0, edge))[b]
            to = (0, edge, edge + GROUP)[b]
            xn = ref[pl.ds(o * GROUP + first, count), :]
            npos = base + (b - 1) * ROWS + DIL * (iota((count, 1), 0) + first) + o
            nseg = segment_of(npos, near_ends)
            ndst = pl.ds(to, count)
            kn_ref[o, ndst, :] = (
                dot(xn, wk_ref[:, near_cols]) + tiled(key_marks(nseg))
            ).astype(BF16)
            vn_ref[o, ndst, :] = (dot(xn, wv_ref[:, near_cols]) + ones_lane[:count]).astype(BF16)
            if b == 1:
                qm_ref[0, rows, :] = query_marks(nseg).astype(BF16)

    def near_block(b, carry):
        g = pl.multiple_of(b * 32, 32)
        q = jnp.concatenate(
            [q_ref[pl.ds(o * GROUP + g, 32), near_cols] for o in range(DIL)], axis=0
        )
        m = jnp.concatenate([qm_ref[0, pl.ds(o * GROUP + g, 32), :] for o in range(DIL)], axis=0)
        k = jnp.concatenate([kn_ref[o, pl.ds(g, 160), :] for o in range(DIL)], axis=0)
        v = jnp.concatenate([vn_ref[o, pl.ds(g, 160), :] for o in range(DIL)], axis=0)
        out = attend(q, m, k, v)
        for o in range(DIL):
            ctx_ref[pl.ds(o * GROUP + g, 32), near_cols] = out[o * 32 : (o + 1) * 32, :]
        return carry

    lax.fori_loop(0, ROWS // 128, near_block, 0)

    def far_block(i, carry):
        o, half = i // 2, i % 2
        g = pl.multiple_of(half * 128, 128)
        rows = pl.ds(o * GROUP + g, 128)
        k = kf_ref[o, pl.ds(g, 640), :]
        v = vf_ref[o, pl.ds(g, 640), :]
        ctx_ref[rows, far_cols] = attend(q_ref[rows, far_cols], qm_ref[1, rows, :], k, v)
        return carry

    lax.fori_loop(0, ROWS // 128, far_block, 0)

    for o in range(DIL):
        rows = pl.ds(o * GROUP, GROUP)
        out = start_ref[rows, :].astype(F32) + dot(ctx_ref[rows, :], wo_ref[...])
        nat_ref[rows, :] = out.astype(BF16)
    step = 256
    for k in range(ROWS // step):
        r = iota((step, ROWS), 0) + k * step
        pick = jnp.where(
            iota((step, ROWS), 1) == (r % DIL) * GROUP + r // DIL, 1.0, 0.0
        ).astype(BF16)
        feat_ref[pl.ds(k * step, step), :] = dot(pick, nat_ref[...]).astype(BF16)
    sel = jnp.where(iota((8, ROWS), 0) == iota((8, ROWS), 1) // REGION, tissue_ref[...], 0)
    pooled = dot(sel.astype(BF16), feat_ref[...]) / REGION
    pool_ref[...] = pooled


AXES = ("x", "y", "z")


def region_kernel(pool_ref, hosp_ref, wk_ref, stat_ref, grad_ref, pair_ref, half_ref, full_ref, np_ref, ps, pr, ss, rs, cs, cr):
    enc, reg = lax.axis_index("enc"), lax.axis_index("region")
    core = reg % 2
    at = {"z": enc, "x": (reg // 2) % 4, "y": reg // 8}

    def device(shift):
        c = {a: (at[a] + shift.get(a, 0)) % 4 for a in AXES}
        return (c["z"], (c["y"] * 4 + c["x"]) * 2 + (core + shift.get("core", 0)) % 2)

    barrier = pltpu.get_barrier_semaphore()
    partners = [{"core": 1}] + [{a: k} for a in AXES for k in (1, 2, 3)]
    for shift in partners:
        pl.semaphore_signal(barrier, inc=1, device_id=device(shift), device_id_type=MESH)

    pooled = pool_ref[...]
    center = pooled - jnp.mean(pooled, axis=1, keepdims=True)
    var = jnp.mean(center * center, axis=1, keepdims=True)
    norm = center * lax.rsqrt(var + EPS)
    row = iota((8, D), 0)
    norm = jnp.where(row < 4, norm, 0.0)
    swapped = jnp.concatenate([norm[4:], norm[:4]], axis=0)
    pair_ref[0] = jnp.where(core == 0, norm, swapped)
    pl.semaphore_wait(barrier, len(partners))
    first = pltpu.make_async_remote_copy(
        src_ref=pair_ref.at[0], dst_ref=pair_ref.at[1], send_sem=ps, recv_sem=pr,
        device_id=device({"core": 1}), device_id_type=MESH,
    )
    first.start()
    first.wait()
    chip = pair_ref[0] + pair_ref[1]
    mine = jnp.where(core == 0, chip[:, :HALF], chip[:, HALF:])
    orders = [("z", "y", "x"), ("y", "x", "z"), ("x", "z", "y")]

    def offset(order):
        return ((at[order[2]] * 4 + at[order[1]]) * 4 + at[order[0]]) * 8

    for t, order in enumerate(orders):
        start = pl.multiple_of(offset(order), 8)
        half_ref[t, pl.ds(start, 8), :] = mine[:, t * LANES : (t + 1) * LANES]
    size = 8
    for stage in range(3):
        copies = []
        for t, order in enumerate(orders):
            start = pl.multiple_of(offset(order) // size * size, size)
            for k in (1, 2, 3):
                window = half_ref.at[t, pl.ds(start, size), :]
                copies.append(
                    pltpu.make_async_remote_copy(
                        src_ref=window, dst_ref=window,
                        send_sem=ss.at[stage, t, k - 1], recv_sem=rs.at[stage, t, k - 1],
                        device_id=device({order[stage]: k}), device_id_type=MESH,
                    )
                )
        for c in copies:
            c.start()
        for c in copies:
            c.wait()
        size *= 4
    last = pltpu.make_async_remote_copy(
        src_ref=half_ref, dst_ref=full_ref, send_sem=cs, recv_sem=cr,
        device_id=device({"core": 1}), device_id_type=MESH,
    )
    last.start()
    last.wait()

    for x in range(4):
        for y in range(4):
            for z in range(4):
                i = {"x": x, "y": y, "z": z}
                to = pl.ds(((x * 4 + y) * 4 + z) * 8, 8)
                for t, order in enumerate(orders):
                    src = pl.ds(((i[order[2]] * 4 + i[order[1]]) * 4 + i[order[0]]) * 8, 8)
                    a, b = half_ref[t, src, :], full_ref[t, src, :]
                    np_ref[to, t * LANES : (t + 1) * LANES] = jnp.where(core == 0, a, b)
                    np_ref[to, HALF + t * LANES : HALF + (t + 1) * LANES] = jnp.where(core == 0, b, a)

    n = PEERS * 4
    hp = lax.Precision.HIGHEST
    hosp = hosp_ref[...]
    ones = jnp.sum(hosp).astype(F32)
    per_slide = float(n // NENC)
    count_one = ones * per_slide
    count_zero = (NENC - ones) * per_slide

    def weights(slide, axis):
        label = jnp.zeros(slide.shape, I32)
        for s in range(NENC):
            label = jnp.where(slide == s, hosp[:, s : s + 1], label)
        return jnp.where(label == 1, 1.0 / count_one, -1.0 / count_zero)

    w_col = weights((iota((n, 1), 0) // 8) % 4, 0)
    w_row = weights((iota((1, n), 1) // 8) % 4, 1)
    normal = np_ref[...]
    emb = jnp.dot(normal, wk_ref[...], precision=hp, preferred_element_type=F32)
    sq = emb * emb
    sq_col = jnp.sum(sq, axis=1, keepdims=True)
    sq_row = lax.dot_general(
        jnp.ones((8, sq.shape[1]), F32), sq, (((1,), (1,)), ((), ())), precision=hp,
        preferred_element_type=F32,
    )[0:1, :]
    inner = lax.dot_general(
        emb, emb, (((1,), (1,)), ((), ())), precision=hp, preferred_element_type=F32
    )
    kern = jnp.exp(-(sq_col + sq_row - 2.0 * inner) / (2.0 * emb.shape[1])) * w_row
    sums = jnp.sum(kern, axis=1, keepdims=True)
    moments = jnp.dot(kern, emb, precision=hp, preferred_element_type=F32)
    stat = n * jnp.sum(w_col * sums)
    stat_ref[...] = jnp.zeros((8, LANES), F32) + stat
    g = (-2.0 * n / emb.shape[1]) * w_col * (sums * emb - moments)
    grad_ref[...] = 100.0 * lax.dot_general(
        normal, g, (((0,), (0,)), ((), ())), precision=hp, preferred_element_type=F32
    )


def pair_columns(w):
    w = w.reshape(w.shape[0], PAIRS, 2 * HEAD)
    return jnp.pad(w, ((0, 0), (0, 0), (0, LANES - 2 * HEAD))).reshape(w.shape[0], PAIRS * LANES)


def local(
    embeddings, tile_position, w_in, ln_gain, w_query, w_key, w_value, w_out,
    near_lengths, far_lengths, tissue, hospital, w_kernel,
):
    sds = jax.ShapeDtypeStruct
    xs, ps = pl.pallas_call(
        project_kernel,
        out_shape=(sds((2 * ROWS, HALF), BF16), sds((PEERS, 1, LANES), F32)),
        in_specs=[VM] * 3,
        out_specs=(VM, VM),
        scratch_shapes=[pltpu.VMEM((ROWS, D), BF16)],
        compiler_params=params(),
        name="project",
    )(embeddings, tile_position.reshape(1, ROWS), w_in)
    xr, pr = pl.pallas_call(
        exchange_kernel,
        out_shape=(sds((2 * ROWS, HALF), BF16), sds((PEERS, 1, LANES), F32)),
        in_specs=[VM] * 2,
        out_specs=(VM, VM),
        scratch_shapes=[pltpu.SemaphoreType.DMA] * 4 + [pltpu.SemaphoreType.DMA((2,))],
        compiler_params=params(collective_id=0, has_side_effects=True),
        name="exchange",
    )(xs, ps)
    start, normed = pl.pallas_call(
        land_kernel,
        out_shape=(sds((ROWS, D), BF16), sds((ROWS, D), BF16)),
        in_specs=[VM] * 3,
        out_specs=(VM, VM),
        scratch_shapes=[pltpu.VMEM((ROWS, D), BF16)],
        compiler_params=params(),
        name="land",
    )(xr, pr, ln_gain.reshape(1, D))
    up = [(i, i + 1) for i in range(NREGION - 1)]
    down = [(i + 1, i) for i in range(NREGION - 1)]
    left = lax.ppermute(normed, "region", up)
    right = lax.ppermute(normed, "region", down)

    wo = jnp.pad(
        w_out.reshape(PAIRS, 2 * HEAD, D), ((0, 0), (0, LANES - 2 * HEAD), (0, 0))
    ).reshape(PAIRS * LANES, D)
    features, pooled = pl.pallas_call(
        layer_kernel,
        out_shape=(sds((ROWS, D), BF16), sds((8, D), F32)),
        in_specs=[VM] * 11,
        out_specs=(VM, VM),
        scratch_shapes=[
            pltpu.VMEM((ROWS, 2 * PW), BF16),
            pltpu.VMEM((2, ROWS, LANES), BF16),
            pltpu.VMEM((DIL, GROUP + 128, PW), BF16),
            pltpu.VMEM((DIL, GROUP + 128, PW), BF16),
            pltpu.VMEM((DIL, 3 * GROUP, PW), BF16),
            pltpu.VMEM((DIL, 3 * GROUP, PW), BF16),
            pltpu.VMEM((ROWS, 2 * PW), BF16),
            pltpu.VMEM((ROWS, D), BF16),
        ],
        compiler_params=params(),
        name="layer",
    )(
        start, normed, left, right, pair_columns(w_query), pair_columns(w_key),
        pair_columns(w_value), wo, near_lengths, far_lengths, tissue.reshape(1, ROWS),
    )
    stat, grad = pl.pallas_call(
        region_kernel,
        out_shape=(sds((8, LANES), F32), sds((D, 256), F32)),
        in_specs=[VM] * 3,
        out_specs=(VM, VM),
        scratch_shapes=[
            pltpu.VMEM((2, 8, D), F32),
            pltpu.VMEM((3, 512, LANES), F32),
            pltpu.VMEM((3, 512, LANES), F32),
            pltpu.VMEM((512, D), F32),
            pltpu.SemaphoreType.DMA,
            pltpu.SemaphoreType.DMA,
            pltpu.SemaphoreType.DMA((3, 3, 3)),
            pltpu.SemaphoreType.DMA((3, 3, 3)),
            pltpu.SemaphoreType.DMA,
            pltpu.SemaphoreType.DMA,
        ],
        compiler_params=params(collective_id=1, has_side_effects=True),
        name="regions",
    )(pooled, hospital.reshape(1, NENC), w_kernel)
    return features, stat[0, 0], grad


def solution(mesh):
    split = P(("enc", "region"))
    return jax.shard_map(
        local,
        mesh=mesh,
        in_specs=(
            P(("enc", "region"), None), split, P(), P(), P(), P(), P(), P(), P(), P(), split, P(), P(),
        ),
        out_specs=(P(("enc", "region"), None), P(), P()),
        check_vma=False,
    )
```

time: 479 us -> 177 us (0.37); the launches traced: 473 us -> 177 us
  Pallas kernels: 0 us -> 149 us
  blocking collectives: 105 us -> 0 us
  waiting for transfers between devices: 112 us -> 7.18 us
  matrix products: 84.8 us -> 0 us
  local copies, waits for them, and re-layouts: 96.9 us -> 14.9 us
  starting transfers between devices: 33.1 us -> 5.55 us
  other arithmetic: 25.6 us -> 0 us
  between operations: 16.5 us -> 0.73 us
    pallas_call x0 -> x5, Pallas kernels: none -> 149 us  [the longest x1 63.4 us: local(): pl.pallas_call(layer_kernel, out_shape=(sds((ROWS, D), BF16), sds((8, D),...]
    psum x1 -> x0, waiting for transfers between devices: 78.6 us -> none  [local(): statistic, kernel_grad = lax.psum((stat_part, grad_part), ('enc', 'region'))]
    psum x1 -> x0, blocking collectives: 64.7 us -> none  [local(): statistic, kernel_grad = lax.psum((stat_part, grad_part), ('enc', 'region'))]
    dot_general x12 -> x0, matrix products: 45.5 us -> none  [the longest x2 24.8 us: attend(): jnp.einsum('bhqk,bkhe->bqhe', weights, values, preferred_element_type=jnp...]
    all_gather x1 -> x0, blocking collectives: 40.2 us -> none  [local(): piece = lax.all_gather(embedded, ('enc', 'region'), axis=0, tiled=True)]
    sub x2 -> x0, matrix products: 39.3 us -> none  [attend(): exponent = jnp.where(allowed, jnp.exp(masked - row_peak), 0.0)]
    another operation x7 -> x0, local copies, waits for them, and re-layouts: 35.5 us -> none  [the longest x2 17.4 us: block_context(): far_kv[1].reshape(3 * group_rows, DILATION, head_count, head_size)]
    all_to_all x2 -> x0, waiting for transfers between devices: 29.5 us -> none  [the longest x1 29.5 us: local(): lax.all_to_all(payload.reshape(senders, per_peer, width_sent), ('enc', 'r...]
  transfers between devices with their start and end apart: 7 -> 2, of which waited for: 4 -> 2; matrix products, arithmetic and copies ran while one was open for 18% -> 6% of each run, Pallas kernels for 0% -> 0%
where the time goes in v1:
time: 177 us
  Pallas kernels  149 us (84%)
  local copies, waits for them, and re-layouts  14.9 us (8%)
  waiting for transfers between devices  7.18 us (4%)
  starting transfers between devices  5.55 us (3%)
    pallas_call x1, Pallas kernels, local(): pl.pallas_call(layer_kernel, out_shape=(sds((ROWS, D), BF16), sds((8, D),...  63.4 us
    pallas_call x1, Pallas kernels, local(): pl.pallas_call(exchange_kernel, out_shape=(sds((2 * ROWS, HALF), BF16), s...  37.8 us
    pallas_call x1, Pallas kernels, local(): pl.pallas_call(region_kernel, out_shape=(sds((8, LANES), F32), sds((D, 25...  33.5 us
    pallas_call x1, Pallas kernels, local(): pl.pallas_call(project_kernel, out_shape=(sds((2 * ROWS, HALF), BF16), sd...  8.6 us
    ppermute x1, waiting for transfers between devices, local(): right = lax.ppermute(normed, 'region', down)  6 us
    unnamed x8, local copies, waits for them, and re-layouts  5.85 us
    pallas_call x1, Pallas kernels, local(): pl.pallas_call(land_kernel, out_shape=(sds((ROWS, D), BF16), sds((ROWS, D...  5.25 us
    reshape x3, local copies, waits for them, and re-layouts, pair_columns(): jnp.pad(w, ((0, 0), (0, 0), (0, LANES - 2 * HEAD)))  5 us
  transfers between devices with their start and end apart: 2, of which 2 were waited for; matrix products, arithmetic and copies ran while one was open for 6% of the time, Pallas kernels for 0%

profile of v1, /device:TPU:1, one launch (start us, length us, event | category | flops | bytes accessed | tf_op | source)
XLA Modules:
  0.0 177.0 jit_solution(7219121595340208995)
XLA Ops:
  0.6 1.3 reshape.43.gain_ref
  1.9 8.6 %project.1 = (bf16[2048,384]{1,0:T(8,128)(2,1)}, f32[128,1,128]{2,1,0:T(1,128)}) custom-call(bf16[1024,1536]{1,0:T(8,128)(2,1)} %emb_ref.1, s32[1,1024]{1,0:T(1,128)} %bitcast.20, bf16[1536,768]{1,0:T(8,128)(2,1)} %w_ref.1), custom_call_target="tpu_custom_call" | custom-call | tf_op jit(solution)/shard_map/project/pallas_call | solution.py:414
  10.5 0.0 copy-start
  10.5 37.8 %exchange.1 = (bf16[2048,384]{1,0:T(8,128)(2,1)}, f32[128,1,128]{2,1,0:T(1,128)}) custom-call(bf16[2048,384]{1,0:T(8,128)(2,1)} %get-tuple-element.13.xs_ref, f32[128,1,128]{2,1,0:T(1,128)} %get-tuple-element.14.ps_ref), custom_call_target="tpu_custom_call" | custom-call | tf_op jit(solution)/shard_map/exchange/pallas_call | solution.py:423
  48.3 5.2 %land.1 = (bf16[1024,768]{1,0:T(8,128)(2,1)}, bf16[1024,768]{1,0:T(8,128)(2,1)}) custom-call(bf16[2048,384]{1,0:T(8,128)(2,1)} %get-tuple-element.15.xr_ref, f32[128,1,128]{2,1,0:T(1,128)} %get-tuple-element.16.pr_ref, bf16[1,768]{1,0:T(2,128)(2,1)} %reshape.43.gain_ref), custom_call_target="tpu_custom_call" | custom-call | tf_op jit(solution)/shard_map/land/pallas_call | solution.py:432
  53.6 2.3 %collective-permute-start.1 = (bf16[1024,768]{1,0:T(8,128)(2,1)}, bf16[1024,768]{1,0:T(8,128)(2,1)}, u32[]{:S(2)}, u32[]{:S(2)}) collective-permute-start(bf16[1024,768]{1,0:T(8,128)(2,1)} %get-tuple-element.18.own_ref), channel_id=1, source_target_pairs={{1,0},{2,1},{3,2},{4,3},{5,4},{6,5},{7,6},{8,7},{9,8},{10,9},{11,1... | collective-permute-start | bytes 4718600 | tf_op jit(solution)/shard_map/ppermute | solution.py:444
  55.9 3.3 %collective-permute-start = (bf16[1024,768]{1,0:T(8,128)(2,1)}, bf16[1024,768]{1,0:T(8,128)(2,1)}, u32[]{:S(2)}, u32[]{:S(2)}) collective-permute-start(bf16[1024,768]{1,0:T(8,128)(2,1)} %get-tuple-element.18.own_ref), channel_id=1, source_target_pairs={{0,1},{1,2},{2,3},{3,4},{4,5},{5,6},{6,7},{7,8},{8,9},{9,10},{10,1... | collective-permute-start | bytes 4718600 | tf_op jit(solution)/shard_map/ppermute | solution.py:443
  59.2 0.0 copy-done
  59.2 0.6 copy.16
  59.8 0.1 pad.14
  59.9 1.6 copy.22.wq_ref
  61.6 1.6 copy.18
  63.1 0.1 pad.15
  63.3 1.7 copy.23.wk_ref
  65.0 1.6 copy.20
  66.6 0.1 pad.16
  66.7 0.0 copy-start.1
  66.7 1.7 copy.24.wv_ref
  68.3 0.0 copy-done.1
  68.3 1.3 pad.17
  69.6 6.0 %collective-permute-done.1.right_ref = bf16[1024,768]{1,0:T(8,128)(2,1)} collective-permute-done((bf16[1024,768]{1,0:T(8,128)(2,1)}, bf16[1024,768]{1,0:T(8,128)(2,1)}, u32[]{:S(2)}, u32[]{:S(2)}) %collective-permute-start.1) | collective-permute-done | bytes 1572896 | tf_op jit(solution)/shard_map/ppermute | solution.py:444
  75.6 1.2 collective-permute-done.left_ref
  76.8 63.4 %layer.1 = (bf16[1024,768]{1,0:T(8,128)(2,1)}, f32[8,768]{1,0:T(8,128)}) custom-call(bf16[1024,768]{1,0:T(8,128)(2,1)} %get-tuple-element.17.start_ref, bf16[1024,768]{1,0:T(8,128)(2,1)} %get-tuple-element.18.own_ref, bf16[1024,768]{1,0:T(8,128)(2,1)} %collective-permute-done.left_ref, bf16[1024,768]{1,0:T(8,128)(2,1)} %collective-permute-done.1.right_ref, ...), custom_call_target="tpu_custom_call" | custom-call | tf_op jit(solution)/shard_map/layer/pallas_call | solution.py:449
  140.2 33.5 %regions.1 = (f32[8,128]{1,0:T(8,128)}, f32[768,256]{1,0:T(8,128)}) custom-call(f32[8,768]{1,0:T(8,128)} %get-tuple-element.20.pool_ref, s32[1,4]{1,0:T(1,128)} %bitcast.22, f32[768,256]{1,0:T(8,128)} %wk_ref.1), custom_call_target="tpu_custom_call" | custom-call | tf_op jit(solution)/shard_map/regions/pallas_call | solution.py:470
  173.7 1.2 slice.3
  174.9 2.1 %copy.26 = f32[768,256]{1,0:T(8,128)} copy(f32[768,256]{1,0:T(8,128)} %get-tuple-element.28) | data formatting | bytes 1572864
Async XLA Ops:
  10.5 48.7 %copy-start = (bf16[768,768]{1,0:T(8,128)(2,1)S(1)}, bf16[768,768]{1,0:T(8,128)(2,1)}, u32[]{:S(2)}) copy-start(bf16[768,768]{1,0:T(8,128)(2,1)} %param.17) | copy-start | bytes 3538948
  53.6 22.0 %collective-permute-start.1 = (bf16[1024,768]{1,0:T(8,128)(2,1)}, bf16[1024,768]{1,0:T(8,128)(2,1)}, u32[]{:S(2)}, u32[]{:S(2)}) collective-permute-start(bf16[1024,768]{1,0:T(8,128)(2,1)} %get-tuple-element.18.own_ref), channel_id=1, source_target_pairs={{1,0},{2,1},{3,2},{4,3},{5,4},{6,5},{7,6},{8,7},{9,8},{10,9},{11,1... | collective-permute-start | bytes 4718600 | tf_op jit(solution)/shard_map/ppermute | solution.py:444
  55.9 20.9 %collective-permute-start = (bf16[1024,768]{1,0:T(8,128)(2,1)}, bf16[1024,768]{1,0:T(8,128)(2,1)}, u32[]{:S(2)}, u32[]{:S(2)}) collective-permute-start(bf16[1024,768]{1,0:T(8,128)(2,1)} %get-tuple-element.18.own_ref), channel_id=1, source_target_pairs={{0,1},{1,2},{2,3},{3,4},{4,5},{5,6},{6,7},{7,8},{8,9},{9,10},{10,1... | collective-permute-start | bytes 4718600 | tf_op jit(solution)/shard_map/ppermute | solution.py:443
  66.7 1.7 copy-start.1

commit v2 on v1

--- a/solution.py
+++ b/solution.py
@@ -26,6 +26,7 @@
 NREGION = 32
 PEERS = NENC * NREGION
 CAP = 8
+SPREAD = 45
 HALF = D // 2
 EPS = 1e-05
 BIG = 1e30
@@ -50,7 +51,24 @@
 VM = pl.BlockSpec(memory_space=pltpu.VMEM)
 
 
-def project_kernel(emb_ref, pos_ref, w_ref, xs_ref, ps_ref, s_ref):
+def handoff_kernel(
+    emb_ref, pos_ref, w_ref, gain_ref, wq_ref, wk_ref, wv_ref, wo_ref,
+    start_ref, normed_ref, wq_out, wk_out, wv_out, wo_out,
+    s_ref, tab_ref, xs_ref, ps_ref, xr_ref, pr_ref, sx, rx, sp, rp, own,
+):
+    me = lax.axis_index("enc") * NREGION + lax.axis_index("region")
+    chunk = 2 * CAP
+    barrier = pltpu.get_barrier_semaphore()
+
+    def signal(k, carry):
+        peer = (me + k) % PEERS
+        pl.semaphore_signal(
+            barrier, inc=1, device_id=(peer // NREGION, peer % NREGION), device_id_type=MESH
+        )
+        return carry
+
+    lax.fori_loop(1, PEERS, signal, 0)
+
     pos = pos_ref[...].astype(F32)
     eye = iota((LANES, LANES), 0) == iota((LANES, LANES), 1)
     rank = jnp.zeros((1, ROWS), F32)
@@ -67,8 +85,13 @@
     for c in range(CAP):
         hit = jnp.where(dest + c == rank, slot, 0.0)
         table = jnp.where(lane == c, jnp.sum(hit, axis=1, keepdims=True), table)
-    for d in range(PEERS):
-        ps_ref[d] = table[d : d + 1, :]
+    tab_ref[...] = table
+
+    def spill(d, carry):
+        ps_ref[d] = tab_ref[pl.ds(d, 1), :]
+        return carry
+
+    lax.fori_loop(0, PEERS, spill, 0)
     step = 256
     for k in range(ROWS // step):
         s_ref[pl.ds(k * step, step), :] = dot(
@@ -80,20 +103,6 @@
         both = jnp.concatenate([moved[:, :, :HALF], moved[:, :, HALF:]], axis=1)
         xs_ref[pl.ds(k * 2 * step, 2 * step), :] = both.reshape(2 * step, HALF).astype(BF16)
 
-
-def exchange_kernel(xs_ref, ps_ref, xr_ref, pr_ref, sx, rx, sp, rp, own):
-    me = lax.axis_index("enc") * NREGION + lax.axis_index("region")
-    chunk = 2 * CAP
-    barrier = pltpu.get_barrier_semaphore()
-
-    def signal(k, carry):
-        peer = (me + k) % PEERS
-        pl.semaphore_signal(
-            barrier, inc=1, device_id=(peer // NREGION, peer % NREGION), device_id_type=MESH
-        )
-        return carry
-
-    lax.fori_loop(1, PEERS, signal, 0)
     mine_x = pltpu.make_async_copy(
         xs_ref.at[pl.ds(me * chunk, chunk), :], xr_ref.at[pl.ds(me * chunk, chunk), :], own.at[0]
     )
@@ -103,7 +112,7 @@
     pl.semaphore_wait(barrier, PEERS - 1)
 
     def send(k, carry):
-        peer = (me + k) % PEERS
+        peer = (me + k * SPREAD) % PEERS
         where = (peer // NREGION, peer % NREGION)
         pltpu.make_async_remote_copy(
             src_ref=ps_ref.at[peer], dst_ref=pr_ref.at[me],
@@ -117,18 +126,29 @@
         return carry
 
     lax.fori_loop(1, PEERS, send, 0)
+
+    gap = jnp.zeros((D, LANES - 2 * HEAD), BF16)
+    for src, dst in ((wq_ref, wq_out), (wk_ref, wk_out), (wv_ref, wv_out)):
+        for j in range(PAIRS):
+            pair = src[:, 2 * HEAD * j : 2 * HEAD * (j + 1)]
+            dst[:, LANES * j : LANES * (j + 1)] = jnp.concatenate([pair, gap], axis=1)
+    for j in range(PAIRS):
+        wo_out[pl.ds(LANES * j, 2 * HEAD), :] = wo_ref[pl.ds(2 * HEAD * j, 2 * HEAD), :]
+        wo_out[pl.ds(LANES * j + 2 * HEAD, LANES - 2 * HEAD), :] = jnp.zeros((LANES - 2 * HEAD, D), BF16)
+
     mine_x.wait()
     mine_p.wait()
     rest_x = pl.ds(0, (PEERS - 1) * chunk)
     rest_p = pl.ds(0, PEERS - 1)
     pltpu.make_async_copy(ps_ref.at[rest_p], pr_ref.at[rest_p], rp).wait()
     pltpu.make_async_copy(ps_ref.at[rest_p], pr_ref.at[rest_p], sp).wait()
-    pltpu.make_async_copy(xs_ref.at[rest_x, :], xr_ref.at[rest_x, :], rx).wait()
-    pltpu.make_async_copy(xs_ref.at[rest_x, :], xr_ref.at[rest_x, :], sx).wait()
-
-
-def land_kernel(xr_ref, pr_ref, gain_ref, start_ref, normed_ref, x_ref):
-    table = jnp.concatenate([pr_ref[d] for d in range(PEERS)], axis=0)
+
+    def fill(d, carry):
+        tab_ref[pl.ds(d, 1), :] = pr_ref[d]
+        return carry
+
+    lax.fori_loop(0, PEERS, fill, 0)
+    table = tab_ref[...]
     high = jnp.floor(table * (1.0 / 32.0))
     low = table - 32.0 * high
     spread = jnp.where(
@@ -136,17 +156,19 @@
     ).astype(BF16)
     wide = 32.0 * dot(high.astype(BF16), spread) + dot(low.astype(BF16), spread)
     mine = iota((PEERS, ROWS), 0) == iota((PEERS, ROWS), 1) // CAP
-    slot = jnp.sum(jnp.where(mine, wide, 0.0), axis=0, keepdims=True).astype(I32)
-    step = 256
+    place = jnp.sum(jnp.where(mine, wide, 0.0), axis=0, keepdims=True).astype(I32)
+
+    pltpu.make_async_copy(xs_ref.at[rest_x, :], xr_ref.at[rest_x, :], rx).wait()
+    pltpu.make_async_copy(xs_ref.at[rest_x, :], xr_ref.at[rest_x, :], sx).wait()
     for k in range(ROWS // step):
         got = xr_ref[pl.ds(k * 2 * step, 2 * step), :].astype(F32)
         got = got.reshape(step // CAP, 2 * CAP, HALF)
         both = jnp.concatenate([got[:, :CAP, :], got[:, CAP:, :]], axis=2)
-        x_ref[pl.ds(k * step, step), :] = both.reshape(step, D).astype(BF16)
+        s_ref[pl.ds(k * step, step), :] = both.reshape(step, D).astype(BF16)
     gain = gain_ref[...].astype(F32)
     for k in range(ROWS // step):
-        pick = jnp.where(iota((step, ROWS), 0) + k * step == slot, 1.0, 0.0).astype(BF16)
-        rows = dot(pick, x_ref[...])
+        pick = jnp.where(iota((step, ROWS), 0) + k * step == place, 1.0, 0.0).astype(BF16)
+        rows = dot(pick, s_ref[...])
         start_ref[pl.ds(k * step, step), :] = rows.astype(BF16)
         center = rows - jnp.mean(rows, axis=1, keepdims=True)
         var = jnp.mean(center * center, axis=1, keepdims=True)
@@ -181,33 +203,67 @@
     return jnp.where((lane >= 0) & (lane < 2 * BITS), mark, 0).astype(F32) * -BIG
 
 
-def attend(queries, marks, keys, values):
-    n = queries.shape[0]
+def attend(query, marks, key, value):
+    n = marks.shape[0]
     lane = iota((n, LANES), 1)
+    pairs = range(PAIRS // 2)
+    scores = []
+    for j in pairs:
+        both = query(j)
+        q = jnp.concatenate(
+            [
+                jnp.where((lane >= h * HEAD) & (lane < (h + 1) * HEAD), both, marks)
+                for h in range(2)
+            ],
+            axis=0,
+        )
+        scores.append(
+            lax.dot_general(q, key(j), (((1,), (1,)), ((), ())), preferred_element_type=F32)
+        )
+    probs = [
+        jnp.exp2((s - jnp.max(s, axis=1, keepdims=True)) * EXP_SCALE).astype(BF16) for s in scores
+    ]
     out = []
-    for j in range(PAIRS // 2):
-        cols = slice(j * LANES, (j + 1) * LANES)
-        both = queries[:, cols]
-        kk, vv = keys[:, cols], values[:, cols]
-        parts = []
-        for h in range(2):
-            q = jnp.where((lane >= h * HEAD) & (lane < (h + 1) * HEAD), both, marks)
-            s = lax.dot_general(q, kk, (((1,), (1,)), ((), ())), preferred_element_type=F32)
-            peak = jnp.max(s, axis=1, keepdims=True)
-            p = jnp.exp2((s - peak) * EXP_SCALE).astype(BF16)
-            o = dot(p, vv)
-            parts.append(o / o[:, 2 * HEAD : 2 * HEAD + 1])
-        res = jnp.where(lane < HEAD, parts[0], jnp.where(lane < 2 * HEAD, parts[1], 0.0))
-        out.append(res.astype(BF16))
+    for j in pairs:
+        o = dot(probs[j], value(j))
+        o = o / o[:, 2 * HEAD : 2 * HEAD + 1]
+        o = jnp.where(lane < HEAD, o[:n], jnp.where(lane < 2 * HEAD, o[n:], 0.0))
+        out.append(o.astype(BF16))
     return jnp.concatenate(out, axis=1)
 
 
 def layer_kernel(
-    start_ref, own_ref, left_ref, right_ref, wq_ref, wk_ref, wv_ref, wo_ref,
+    start_ref, own_ref, wq_ref, wk_ref, wv_ref, wo_ref,
     near_ref, far_ref, tissue_ref, feat_ref, pool_ref,
-    q_ref, qm_ref, kn_ref, vn_ref, kf_ref, vf_ref, ctx_ref, nat_ref,
+    left_ref, right_ref, q_ref, qm_ref, kn_ref, vn_ref, kf_ref, vf_ref, ctx_ref, nat_ref,
+    send_sem, recv_sem,
 ):
-    base = lax.axis_index("region") * ROWS
+    enc, reg = lax.axis_index("enc"), lax.axis_index("region")
+    after, before = (reg + 1) % NREGION, (reg + NREGION - 1) % NREGION
+    barrier = pltpu.get_barrier_semaphore()
+    for other in (before, after):
+        pl.semaphore_signal(barrier, inc=1, device_id=(enc, other), device_id_type=MESH)
+    pl.semaphore_wait(barrier, 2)
+    edge = GROUP // 4
+    near_copies, far_copies = [], []
+    for kind, copies in ((0, near_copies), (1, far_copies)):
+        for o in range(DIL):
+            for way, dst, other in ((0, left_ref, after), (1, right_ref, before)):
+                first = ((GROUP - edge, 0), (0, edge))[kind][way]
+                rows = pl.ds(o * GROUP + first, (edge, GROUP - edge)[kind])
+                copies.append(
+                    pltpu.make_async_remote_copy(
+                        src_ref=own_ref.at[rows, :], dst_ref=dst.at[rows, :],
+                        send_sem=send_sem.at[kind, way, o], recv_sem=recv_sem.at[kind, way, o],
+                        device_id=(enc, other), device_id_type=MESH,
+                    )
+                )
+    for c in near_copies:
+        c.start()
+    for c in far_copies:
+        c.start()
+
+    base = reg * ROWS
     near_ends = ends_of(near_ref[...])
     far_ends = ends_of(far_ref[...])
     near_cols, far_cols = pl.ds(0, PW), pl.ds(PW, PW)
@@ -216,54 +272,73 @@
     def tiled(marks):
         return jnp.concatenate([marks] * (PAIRS // 2), axis=1)
 
-    edge = GROUP // 4
+    def far_rows(o, b, ref):
+        x = ref[pl.ds(o * GROUP, GROUP), :]
+        seg = segment_of(base + (b - 1) * ROWS + DIL * iota((GROUP, 1), 0) + o, far_ends)
+        dst = pl.ds(b * GROUP, GROUP)
+        kf_ref[o, dst, :] = (dot(x, wk_ref[:, far_cols]) + tiled(key_marks(seg))).astype(BF16)
+        vf_ref[o, dst, :] = (dot(x, wv_ref[:, far_cols]) + ones_lane).astype(BF16)
+        return seg
+
+    def near_rows(o, b, ref):
+        first, count = ((GROUP - edge, edge), (0, GROUP), (0, edge))[b]
+        x = ref[pl.ds(o * GROUP + first, count), :]
+        pos = base + (b - 1) * ROWS + DIL * (iota((count, 1), 0) + first) + o
+        seg = segment_of(pos, near_ends)
+        dst = pl.ds((0, edge, edge + GROUP)[b], count)
+        kn_ref[o, dst, :] = (dot(x, wk_ref[:, near_cols]) + tiled(key_marks(seg))).astype(BF16)
+        vn_ref[o, dst, :] = (dot(x, wv_ref[:, near_cols]) + ones_lane[:count]).astype(BF16)
+        return seg
+
     for o in range(DIL):
         rows = pl.ds(o * GROUP, GROUP)
-        for b, ref in enumerate((left_ref, own_ref, right_ref)):
-            x = ref[rows, :]
-            pos = base + (b - 1) * ROWS + DIL * iota((GROUP, 1), 0) + o
-            seg = segment_of(pos, far_ends)
-            dst = pl.ds(b * GROUP, GROUP)
-            kf_ref[o, dst, :] = (dot(x, wk_ref[:, far_cols]) + tiled(key_marks(seg))).astype(BF16)
-            vf_ref[o, dst, :] = (dot(x, wv_ref[:, far_cols]) + ones_lane).astype(BF16)
-            if b == 1:
-                q_ref[rows, :] = dot(x, wq_ref[...]).astype(BF16)
-                qm_ref[1, rows, :] = query_marks(seg).astype(BF16)
-            first, count = ((GROUP - edge, edge), (0, GROUP), (0, edge))[b]
-            to = (0, edge, edge + GROUP)[b]
-            xn = ref[pl.ds(o * GROUP + first, count), :]
-            npos = base + (b - 1) * ROWS + DIL * (iota((count, 1), 0) + first) + o
-            nseg = segment_of(npos, near_ends)
-            ndst = pl.ds(to, count)
-            kn_ref[o, ndst, :] = (
-                dot(xn, wk_ref[:, near_cols]) + tiled(key_marks(nseg))
-            ).astype(BF16)
-            vn_ref[o, ndst, :] = (dot(xn, wv_ref[:, near_cols]) + ones_lane[:count]).astype(BF16)
-            if b == 1:
-                qm_ref[0, rows, :] = query_marks(nseg).astype(BF16)
+        q_ref[rows, :] = dot(own_ref[rows, :], wq_ref[...]).astype(BF16)
+        qm_ref[0, rows, :] = query_marks(near_rows(o, 1, own_ref)).astype(BF16)
+        qm_ref[1, rows, :] = query_marks(far_rows(o, 1, own_ref)).astype(BF16)
+    for c in near_copies:
+        c.wait()
+    for o in range(DIL):
+        near_rows(o, 0, left_ref)
+        near_rows(o, 2, right_ref)
 
     def near_block(b, carry):
         g = pl.multiple_of(b * 32, 32)
-        q = jnp.concatenate(
-            [q_ref[pl.ds(o * GROUP + g, 32), near_cols] for o in range(DIL)], axis=0
+
+        def joined(ref, n, j):
+            cols = slice(j * LANES, (j + 1) * LANES)
+            return jnp.concatenate([ref[o, pl.ds(g, n), cols] for o in range(DIL)], axis=0)
+
+        def query(j):
+            cols = slice(j * LANES, (j + 1) * LANES)
+            return jnp.concatenate(
+                [q_ref[pl.ds(o * GROUP + g, 32), cols] for o in range(DIL)], axis=0
+            )
+
+        marks = jnp.concatenate(
+            [qm_ref[0, pl.ds(o * GROUP + g, 32), :] for o in range(DIL)], axis=0
         )
-        m = jnp.concatenate([qm_ref[0, pl.ds(o * GROUP + g, 32), :] for o in range(DIL)], axis=0)
-        k = jnp.concatenate([kn_ref[o, pl.ds(g, 160), :] for o in range(DIL)], axis=0)
-        v = jnp.concatenate([vn_ref[o, pl.ds(g, 160), :] for o in range(DIL)], axis=0)
-        out = attend(q, m, k, v)
+        out = attend(query, marks, lambda j: joined(kn_ref, 160, j), lambda j: joined(vn_ref, 160, j))
         for o in range(DIL):
             ctx_ref[pl.ds(o * GROUP + g, 32), near_cols] = out[o * 32 : (o + 1) * 32, :]
         return carry
 
     lax.fori_loop(0, ROWS // 128, near_block, 0)
+    for c in far_copies:
+        c.wait()
+    for o in range(DIL):
+        far_rows(o, 0, left_ref)
+        far_rows(o, 2, right_ref)
 
     def far_block(i, carry):
         o, half = i // 2, i % 2
         g = pl.multiple_of(half * 128, 128)
-        rows = pl.ds(o * GROUP + g, 128)
-        k = kf_ref[o, pl.ds(g, 640), :]
-        v = vf_ref[o, pl.ds(g, 640), :]
-        ctx_ref[rows, far_cols] = attend(q_ref[rows, far_cols], qm_ref[1, rows, :], k, v)
+        rows = pl.ds(pl.multiple_of(o * GROUP + g, 128), 128)
+        ctx_ref[rows, far_cols] = attend(
+            lambda j: q_ref[rows, PW + j * LANES : PW + (j + 1) * LANES],
+            qm_ref[1, rows, :],
+            lambda j: kf_ref[o, pl.ds(g, 640), j * LANES : (j + 1) * LANES],
+            lambda j: vf_ref[o, pl.ds(g, 640), j * LANES : (j + 1) * LANES],
+        )
         return carry
 
     lax.fori_loop(0, ROWS // 128, far_block, 0)
@@ -279,9 +354,10 @@
             iota((step, ROWS), 1) == (r % DIL) * GROUP + r // DIL, 1.0, 0.0
         ).astype(BF16)
         feat_ref[pl.ds(k * step, step), :] = dot(pick, nat_ref[...]).astype(BF16)
-    sel = jnp.where(iota((8, ROWS), 0) == iota((8, ROWS), 1) // REGION, tissue_ref[...], 0)
-    pooled = dot(sel.astype(BF16), feat_ref[...]) / REGION
-    pool_ref[...] = pooled
+    sel = jnp.where(
+        iota((8, ROWS), 0) == iota((8, ROWS), 1) // REGION, tissue_ref[...], 0
+    )
+    pool_ref[...] = dot(sel.astype(F32).astype(BF16), feat_ref[...]) / REGION
 
 
 AXES = ("x", "y", "z")
@@ -401,57 +477,41 @@
     )
 
 
-def pair_columns(w):
-    w = w.reshape(w.shape[0], PAIRS, 2 * HEAD)
-    return jnp.pad(w, ((0, 0), (0, 0), (0, LANES - 2 * HEAD))).reshape(w.shape[0], PAIRS * LANES)
-
-
 def local(
     embeddings, tile_position, w_in, ln_gain, w_query, w_key, w_value, w_out,
     near_lengths, far_lengths, tissue, hospital, w_kernel,
 ):
     sds = jax.ShapeDtypeStruct
-    xs, ps = pl.pallas_call(
-        project_kernel,
-        out_shape=(sds((2 * ROWS, HALF), BF16), sds((PEERS, 1, LANES), F32)),
-        in_specs=[VM] * 3,
-        out_specs=(VM, VM),
-        scratch_shapes=[pltpu.VMEM((ROWS, D), BF16)],
-        compiler_params=params(),
-        name="project",
-    )(embeddings, tile_position.reshape(1, ROWS), w_in)
-    xr, pr = pl.pallas_call(
-        exchange_kernel,
-        out_shape=(sds((2 * ROWS, HALF), BF16), sds((PEERS, 1, LANES), F32)),
-        in_specs=[VM] * 2,
-        out_specs=(VM, VM),
-        scratch_shapes=[pltpu.SemaphoreType.DMA] * 4 + [pltpu.SemaphoreType.DMA((2,))],
+    dma = pltpu.SemaphoreType.DMA
+    rows, padded = sds((ROWS, D), BF16), sds((D, PAIRS * LANES), BF16)
+    start, normed, wq, wk, wv, wo = pl.pallas_call(
+        handoff_kernel,
+        out_shape=(rows, rows, padded, padded, padded, sds((PAIRS * LANES, D), BF16)),
+        in_specs=[VM] * 8,
+        out_specs=(VM,) * 6,
+        scratch_shapes=[
+            pltpu.VMEM((ROWS, D), BF16),
+            pltpu.VMEM((PEERS, LANES), F32),
+            pltpu.VMEM((2 * ROWS, HALF), BF16),
+            pltpu.VMEM((PEERS, 1, LANES), F32),
+            pltpu.VMEM((2 * ROWS, HALF), BF16),
+            pltpu.VMEM((PEERS, 1, LANES), F32),
+            dma, dma, dma, dma, dma((2,)),
+        ],
         compiler_params=params(collective_id=0, has_side_effects=True),
-        name="exchange",
-    )(xs, ps)
-    start, normed = pl.pallas_call(
-        land_kernel,
-        out_shape=(sds((ROWS, D), BF16), sds((ROWS, D), BF16)),
-        in_specs=[VM] * 3,
-        out_specs=(VM, VM),
-        scratch_shapes=[pltpu.VMEM((ROWS, D), BF16)],
-        compiler_params=params(),
-        name="land",
-    )(xr, pr, ln_gain.reshape(1, D))
-    up = [(i, i + 1) for i in range(NREGION - 1)]
-    down = [(i + 1, i) for i in range(NREGION - 1)]
-    left = lax.ppermute(normed, "region", up)
-    right = lax.ppermute(normed, "region", down)
-
-    wo = jnp.pad(
-        w_out.reshape(PAIRS, 2 * HEAD, D), ((0, 0), (0, LANES - 2 * HEAD), (0, 0))
-    ).reshape(PAIRS * LANES, D)
+        name="handoff",
+    )(
+        embeddings, tile_position.reshape(1, ROWS), w_in, ln_gain.reshape(1, D),
+        w_query, w_key, w_value, w_out,
+    )
     features, pooled = pl.pallas_call(
         layer_kernel,
-        out_shape=(sds((ROWS, D), BF16), sds((8, D), F32)),
-        in_specs=[VM] * 11,
+        out_shape=(rows, sds((8, D), F32)),
+        in_specs=[VM] * 9,
         out_specs=(VM, VM),
         scratch_shapes=[
+            pltpu.VMEM((ROWS, D), BF16),
+            pltpu.VMEM((ROWS, D), BF16),
             pltpu.VMEM((ROWS, 2 * PW), BF16),
             pltpu.VMEM((2, ROWS, LANES), BF16),
             pltpu.VMEM((DIL, GROUP + 128, PW), BF16),
@@ -460,13 +520,12 @@
             pltpu.VMEM((DIL, 3 * GROUP, PW), BF16),
             pltpu.VMEM((ROWS, 2 * PW), BF16),
             pltpu.VMEM((ROWS, D), BF16),
+            dma((2, 2, DIL)),
+            dma((2, 2, DIL)),
         ],
-        compiler_params=params(),
+        compiler_params=params(collective_id=2, has_side_effects=True),
         name="layer",
-    )(
-        start, normed, left, right, pair_columns(w_query), pair_columns(w_key),
-        pair_columns(w_value), wo, near_lengths, far_lengths, tissue.reshape(1, ROWS),
-    )
+    )(start, normed, wq, wk, wv, wo, near_lengths, far_lengths, tissue.reshape(1, ROWS))
     stat, grad = pl.pallas_call(
         region_kernel,
         out_shape=(sds((8, LANES), F32), sds((D, 256), F32)),

time: 177 us -> 125 us (0.71)
  Pallas kernels: 149 us -> 118 us
  local copies, waits for them, and re-layouts: 14.9 us -> 6.06 us
  waiting for transfers between devices: 7.18 us -> 0 us
  starting transfers between devices: 5.55 us -> 0 us
    pallas_call x4 -> x2, Pallas kernels: 115 us -> 86.1 us  [the longest x1 44.3 us: local(): pl.pallas_call(handoff_kernel, out_shape=(rows, rows, padded, padded, pad...]
    ppermute x2 -> x0, waiting for transfers between devices: 7.18 us -> none  [the longest x1 6 us: local(): right = lax.ppermute(normed, 'region', down)]
    ppermute x2 -> x0, starting transfers between devices: 5.55 us -> none  [the longest x1 3.26 us: local(): left = lax.ppermute(normed, 'region', up)]
    reshape x3 -> x0, local copies, waits for them, and re-layouts: 5 us -> none  [pair_columns(): jnp.pad(w, ((0, 0), (0, 0), (0, LANES - 2 * HEAD)))]
    unnamed x8 -> x4, local copies, waits for them, and re-layouts: 5.85 us -> 3.61 us
    pallas_call x1, Pallas kernels: 33.5 us -> 31.6 us  [local(): pl.pallas_call(region_kernel, out_shape=(sds((8, LANES), F32), sds((D, 25...]
  transfers between devices with their start and end apart: 2 -> 0, of which waited for: 2 -> 0; matrix products, arithmetic and copies ran while one was open for 6% -> 0% of each run, Pallas kernels for 0% -> 0%
where the time goes in v2:
time: 125 us; the launch traced here: 124 us
  Pallas kernels  118 us (94%)
  local copies, waits for them, and re-layouts  6.06 us (5%)
    pallas_call x1, Pallas kernels, local(): pl.pallas_call(handoff_kernel, out_shape=(rows, rows, padded, padded, pad...  44.3 us
    pallas_call x1, Pallas kernels, local(): pl.pallas_call(layer_kernel, out_shape=(rows, sds((8, D), F32)), in_specs...  41.8 us
    pallas_call x1, Pallas kernels, local(): pl.pallas_call(region_kernel, out_shape=(sds((8, LANES), F32), sds((D, 25...  31.6 us
    unnamed x4, local copies, waits for them, and re-layouts  3.61 us

profile of v2, /device:TPU:1, one launch (start us, length us, event | category | flops | bytes accessed | tf_op | source)
XLA Modules:
  0.0 124.4 jit_solution(7622681363008458967)
XLA Ops:
  0.6 1.3 %reshape.19.gain_ref = bf16[1,768]{1,0:T(2,128)(2,1)} reshape(bf16[768]{0:T(1024)(128)(2,1)} %param.16) | data formatting | bytes 3072 | tf_op jit(solution)/shard_map/reshape | solution.py:504
  1.9 44.3 %handoff.1 = (bf16[1024,768]{1,0:T(8,128)(2,1)}, bf16[1024,768]{1,0:T(8,128)(2,1)}, bf16[768,1024]{1,0:T(8,128)(2,1)}, bf16[768,1024]{1,0:T(8,128)(2,1)}, bf16[7...) custom-call(bf16[1024,1536]{1,0:T(8,128)(2,1)} %emb_ref.1, s32[1,1024]{1,0:T(1,128)} %bitcast.4, bf16[1536,768]{1,0:T(8,128)(2,1)} %w_ref.1, ...), custom_call_target="tpu_custom_call" | custom-call | tf_op jit(solution)/shard_map/handoff/pallas_call | solution.py:487
  46.2 41.8 %layer.1 = (bf16[1024,768]{1,0:T(8,128)(2,1)}, f32[8,768]{1,0:T(8,128)}) custom-call(bf16[1024,768]{1,0:T(8,128)(2,1)} %get-tuple-element.13.start_ref, bf16[1024,768]{1,0:T(8,128)(2,1)} %get-tuple-element.14.own_ref, bf16[768,1024]{1,0:T(8,128)(2,1)} %get-tuple-element.15.wq_ref, bf16[768,1024]{1,0:T(8,128)(2,1)} %get-tuple-element.16.wk_ref, ...), custom_call_target="tpu_custom_call" | custom-call | tf_op jit(solution)/shard_map/layer/pallas_call | solution.py:507
  88.0 31.6 %regions.1 = (f32[8,128]{1,0:T(8,128)}, f32[768,256]{1,0:T(8,128)}) custom-call(f32[8,768]{1,0:T(8,128)} %get-tuple-element.20.pool_ref, s32[1,4]{1,0:T(1,128)} %bitcast.6, f32[768,256]{1,0:T(8,128)} %wk_ref.3), custom_call_target="tpu_custom_call" | custom-call | tf_op jit(solution)/shard_map/regions/pallas_call | solution.py:529
  119.6 1.2 slice.3
  120.8 0.0 copy-start
  120.8 2.7 %copy.18 = bf16[1024,768]{1,0:T(8,128)(2,1)} copy(bf16[1024,768]{1,0:T(8,128)(2,1)} %get-tuple-element.26) | data formatting | bytes 3145728
  123.5 0.0 copy-done
  123.5 0.9 copy.19
Async XLA Ops:
  120.8 2.7 %copy-start = (f32[768,256]{1,0:T(8,128)S(1)}, f32[768,256]{1,0:T(8,128)}, u32[]{:S(2)}) copy-start(f32[768,256]{1,0:T(8,128)} %get-tuple-element.28) | copy-start | bytes 2359300

commit v3 on v2

v3 whole, which is shorter than its diff:
```python
import functools

import jax
import jax.numpy as jnp
from jax import lax
from jax.experimental import pallas as pl
from jax.experimental.pallas import tpu as pltpu
from jax.sharding import PartitionSpec as P

MESH = pl.DeviceIdType.MESH
F32 = jnp.float32
BF16 = jnp.bfloat16
I32 = jnp.int32

ROWS = 1024
DIN = 1536
D = 768
PAIRS = 8
HEAD = 48
LANES = 128
PW = PAIRS // 2 * LANES
GROUP = 256
DIL = 4
REGION = 256
NENC = 4
NREGION = 32
PEERS = NENC * NREGION
CAP = 8
SPREAD = 45
HALF = D // 2
EPS = 1e-05
BIG = 1e30
BITS = 9
PAD_SEG = 511
EXP_SCALE = 1.4426950408889634 / 48.0**0.5
VMEM_LIMIT = 60 * 1024 * 1024


def iota(shape, dim):
    return lax.broadcasted_iota(I32, shape, dim)


def dot(a, b):
    return jnp.dot(a, b, preferred_element_type=F32)


def params(**kw):
    return pltpu.CompilerParams(vmem_limit_bytes=VMEM_LIMIT, **kw)


VM = pl.BlockSpec(memory_space=pltpu.VMEM)
ANY = pl.BlockSpec(memory_space=pl.ANY)


def ends_of(lengths):
    n = lengths.shape[1]
    upto = jnp.where(iota((n, n), 0) <= iota((n, n), 1), 1.0, 0.0).astype(BF16)
    high, low = lengths // 32, lengths % 32
    sums = 32.0 * dot(high.astype(F32).astype(BF16), upto) + dot(low.astype(F32).astype(BF16), upto)
    own = iota(sums.shape, 0) == lax.axis_index("enc")
    return jnp.sum(jnp.where(own, sums, 0.0), axis=0, keepdims=True)


def segment_of(pos, ends):
    seg = jnp.sum(jnp.where(ends <= pos.astype(F32), 1.0, 0.0), axis=1, keepdims=True).astype(I32)
    return jnp.where((pos >= 0) & (pos < ROWS * NREGION), seg, PAD_SEG)


def key_marks(seg):
    lane = iota((seg.shape[0], LANES), 1) - 2 * HEAD
    bit = (seg >> jnp.where(lane >= BITS, lane - BITS, jnp.maximum(lane, 0)) % 16) & 1
    mark = jnp.where(lane < BITS, 1 - bit, bit)
    return jnp.where((lane >= 0) & (lane < 2 * BITS), mark, 0).astype(F32)


def query_marks(seg):
    lane = iota((seg.shape[0], LANES), 1) - 2 * HEAD
    bit = (seg >> jnp.where(lane >= BITS, lane - BITS, jnp.maximum(lane, 0)) % 16) & 1
    mark = jnp.where(lane < BITS, bit, 1 - bit)
    return jnp.where((lane >= 0) & (lane < 2 * BITS), mark, 0).astype(F32) * -BIG


def attend(query, marks, key, value):
    n = marks.shape[0]
    lane = iota((n, LANES), 1)
    pairs = range(PAIRS // 2)
    scores = []
    for j in pairs:
        both = query(j)
        q = jnp.concatenate(
            [
                jnp.where((lane >= h * HEAD) & (lane < (h + 1) * HEAD), both, marks)
                for h in range(2)
            ],
            axis=0,
        )
        scores.append(
            lax.dot_general(q, key(j), (((1,), (1,)), ((), ())), preferred_element_type=F32)
        )
    probs = [
        jnp.exp2((s - jnp.max(s, axis=1, keepdims=True)) * EXP_SCALE).astype(BF16) for s in scores
    ]
    out = []
    for j in pairs:
        o = dot(probs[j], value(j))
        o = o / o[:, 2 * HEAD : 2 * HEAD + 1]
        o = jnp.where(lane < HEAD, o[:n], jnp.where(lane < 2 * HEAD, o[n:], 0.0))
        out.append(o.astype(BF16))
    return jnp.concatenate(out, axis=1)


AXES = ("x", "y", "z")


def dot3(a, b, ca=1, cb=0):
    dims = (((ca,), (cb,)), ((), ()))

    def mul(x, y):
        return lax.dot_general(x, y, dims, preferred_element_type=F32)

    ah, bh = a.astype(BF16), b.astype(BF16)
    al, bl = (a - ah.astype(F32)).astype(BF16), (b - bh.astype(F32)).astype(BF16)
    return mul(ah, bh) + (mul(ah, bl) + mul(al, bh))


def slide_kernel(
    emb_hbm, pos_ref, win_hbm, gain_ref, wq_hbm, wk_hbm, wv_hbm, wo_hbm,
    near_ref, far_ref, tissue_ref, hosp_ref, wkern_hbm,
    feat_hbm, stat_ref, grad_ref,
    emb_ref, w_ref, wq_ref, wk_ref, wv_ref, wo_ref, wkern_ref, wq_out, wk_out, wv_out, wo_out,
    start_ref, normed_ref, s_ref, tab_ref, xs_ref, ps_ref, xr_ref, pr_ref,
    left_ref, right_ref, q_ref, qm_ref, kn_ref, vn_ref, kf_ref, vf_ref, ctx_ref,
    pair_ref, half_ref, full_ref, np_ref,
    load_sem, sx, rx, sp, rp, own, send_sem, recv_sem, ps, pr, ss, rs, cs, cr,
):
    me = lax.axis_index("enc") * NREGION + lax.axis_index("region")
    chunk = 2 * CAP
    barrier = pltpu.get_barrier_semaphore()

    def signal(k, carry):
        peer = (me + k) % PEERS
        pl.semaphore_signal(
            barrier, inc=1, device_id=(peer // NREGION, peer % NREGION), device_id_type=MESH
        )
        return carry

    lax.fori_loop(1, PEERS, signal, 0)
    loads = [
        pltpu.make_async_copy(src, dst, load_sem.at[i])
        for i, (src, dst) in enumerate(
            (
                (emb_hbm, emb_ref), (win_hbm, w_ref), (wq_hbm, wq_ref), (wk_hbm, wk_ref),
                (wv_hbm, wv_ref), (wo_hbm, wo_ref), (wkern_hbm, wkern_ref),
            )
        )
    ]
    for c in loads:
        c.start()

    pos = pos_ref[...].astype(F32)
    eye = iota((LANES, LANES), 0) == iota((LANES, LANES), 1)
    rank = jnp.zeros((1, ROWS), F32)
    for k in range(ROWS // LANES):
        part = pos[:, k * LANES : (k + 1) * LANES]
        col = jnp.sum(jnp.where(eye, part, 0.0), axis=1, keepdims=True)
        rank = rank + jnp.sum(jnp.where(col < pos, 1.0, 0.0), axis=0, keepdims=True)
    rank = rank.astype(I32)
    local = pos_ref[...] % ROWS
    slot = ((local % DIL) * GROUP + local // DIL).astype(F32)
    dest = iota((PEERS, ROWS), 0) * CAP
    lane = iota((PEERS, LANES), 1)
    table = jnp.zeros((PEERS, LANES), F32)
    for c in range(CAP):
        hit = jnp.where(dest + c == rank, slot, 0.0)
        table = jnp.where(lane == c, jnp.sum(hit, axis=1, keepdims=True), table)
    tab_ref[...] = table

    def spill(d, carry):
        ps_ref[d] = tab_ref[pl.ds(d, 1), :]
        return carry

    lax.fori_loop(0, PEERS, spill, 0)
    step = 256
    loads[0].wait()
    loads[1].wait()
    for k in range(ROWS // step):
        s_ref[pl.ds(k * step, step), :] = dot(
            emb_ref[pl.ds(k * step, step), :], w_ref[...]
        ).astype(BF16)
    for k in range(ROWS // step):
        pick = jnp.where(iota((step, ROWS), 0) + k * step == rank, 1.0, 0.0).astype(BF16)
        moved = dot(pick, s_ref[...]).reshape(step // CAP, CAP, D)
        both = jnp.concatenate([moved[:, :, :HALF], moved[:, :, HALF:]], axis=1)
        xs_ref[pl.ds(k * 2 * step, 2 * step), :] = both.reshape(2 * step, HALF).astype(BF16)

    mine_x = pltpu.make_async_copy(
        xs_ref.at[pl.ds(me * chunk, chunk), :], xr_ref.at[pl.ds(me * chunk, chunk), :], own.at[0]
    )
    mine_p = pltpu.make_async_copy(ps_ref.at[me], pr_ref.at[me], own.at[1])
    mine_x.start()
    mine_p.start()
    pl.semaphore_wait(barrier, PEERS - 1)

    def send(k, carry):
        peer = (me + k * SPREAD) % PEERS
        where = (peer // NREGION, peer % NREGION)
        pltpu.make_async_remote_copy(
            src_ref=ps_ref.at[peer], dst_ref=pr_ref.at[me],
            send_sem=sp, recv_sem=rp, device_id=where, device_id_type=MESH,
        ).start()
        pltpu.make_async_remote_copy(
            src_ref=xs_ref.at[pl.ds(peer * chunk, chunk), :],
            dst_ref=xr_ref.at[pl.ds(me * chunk, chunk), :],
            send_sem=sx, recv_sem=rx, device_id=where, device_id_type=MESH,
        ).start()
        return carry

    lax.fori_loop(1, PEERS, send, 0)

    for c in loads[2:]:
        c.wait()
    gap = jnp.zeros((D, LANES - 2 * HEAD), BF16)
    for src, dst in ((wq_ref, wq_out), (wk_ref, wk_out), (wv_ref, wv_out)):
        for j in range(PAIRS):
            pair = src[:, 2 * HEAD * j : 2 * HEAD * (j + 1)]
            dst[:, LANES * j : LANES * (j + 1)] = jnp.concatenate([pair, gap], axis=1)
    for j in range(PAIRS):
        wo_out[pl.ds(LANES * j, 2 * HEAD), :] = wo_ref[pl.ds(2 * HEAD * j, 2 * HEAD), :]
        wo_out[pl.ds(LANES * j + 2 * HEAD, LANES - 2 * HEAD), :] = jnp.zeros((LANES - 2 * HEAD, D), BF16)

    mine_x.wait()
    mine_p.wait()
    rest_x = pl.ds(0, (PEERS - 1) * chunk)
    rest_p = pl.ds(0, PEERS - 1)
    pltpu.make_async_copy(ps_ref.at[rest_p], pr_ref.at[rest_p], rp).wait()
    pltpu.make_async_copy(ps_ref.at[rest_p], pr_ref.at[rest_p], sp).wait()

    def fill(d, carry):
        tab_ref[pl.ds(d, 1), :] = pr_ref[d]
        return carry

    lax.fori_loop(0, PEERS, fill, 0)
    table = tab_ref[...]
    high = jnp.floor(table * (1.0 / 32.0))
    low = table - 32.0 * high
    spread = jnp.where(
        iota((LANES, ROWS), 0) == iota((LANES, ROWS), 1) % CAP, 1.0, 0.0
    ).astype(BF16)
    wide = 32.0 * dot(high.astype(BF16), spread) + dot(low.astype(BF16), spread)
    mine = iota((PEERS, ROWS), 0) == iota((PEERS, ROWS), 1) // CAP
    place = jnp.sum(jnp.where(mine, wide, 0.0), axis=0, keepdims=True).astype(I32)

    pltpu.make_async_copy(xs_ref.at[rest_x, :], xr_ref.at[rest_x, :], rx).wait()
    pltpu.make_async_copy(xs_ref.at[rest_x, :], xr_ref.at[rest_x, :], sx).wait()
    for k in range(ROWS // step):
        got = xr_ref[pl.ds(k * 2 * step, 2 * step), :].astype(F32)
        got = got.reshape(step // CAP, 2 * CAP, HALF)
        both = jnp.concatenate([got[:, :CAP, :], got[:, CAP:, :]], axis=2)
        s_ref[pl.ds(k * step, step), :] = both.reshape(step, D).astype(BF16)
    gain = gain_ref[...].astype(F32).reshape(1, D)
    for k in range(ROWS // step):
        pick = jnp.where(iota((step, ROWS), 0) + k * step == place, 1.0, 0.0).astype(BF16)
        rows = dot(pick, s_ref[...])
        start_ref[pl.ds(k * step, step), :] = rows.astype(BF16)
        center = rows - jnp.mean(rows, axis=1, keepdims=True)
        var = jnp.mean(center * center, axis=1, keepdims=True)
        normed_ref[pl.ds(k * step, step), :] = (center * lax.rsqrt(var + EPS) * gain).astype(BF16)

    enc, reg = lax.axis_index("enc"), lax.axis_index("region")
    after, before = (reg + 1) % NREGION, (reg + NREGION - 1) % NREGION
    edge = GROUP // 4
    near_copies, far_copies = [], []
    for kind, copies in ((0, near_copies), (1, far_copies)):
        for o in range(DIL):
            for way, dst, other in ((0, left_ref, after), (1, right_ref, before)):
                first = ((GROUP - edge, 0), (0, edge))[kind][way]
                rows = pl.ds(o * GROUP + first, (edge, GROUP - edge)[kind])
                copies.append(
                    pltpu.make_async_remote_copy(
                        src_ref=normed_ref.at[rows, :], dst_ref=dst.at[rows, :],
                        send_sem=send_sem.at[kind, way, o], recv_sem=recv_sem.at[kind, way, o],
                        device_id=(enc, other), device_id_type=MESH,
                    )
                )
    for c in near_copies:
        c.start()
    for c in far_copies:
        c.start()

    base = reg * ROWS
    near_ends = ends_of(near_ref[...])
    far_ends = ends_of(far_ref[...])
    near_cols, far_cols = pl.ds(0, PW), pl.ds(PW, PW)
    ones_lane = jnp.where(iota((GROUP, PW), 1) % LANES == 2 * HEAD, 1.0, 0.0)

    def tiled(marks):
        return jnp.concatenate([marks] * (PAIRS // 2), axis=1)

    def far_rows(o, b, ref):
        x = ref[pl.ds(o * GROUP, GROUP), :]
        seg = segment_of(base + (b - 1) * ROWS + DIL * iota((GROUP, 1), 0) + o, far_ends)
        dst = pl.ds(b * GROUP, GROUP)
        kf_ref[o, dst, :] = (dot(x, wk_out[:, far_cols]) + tiled(key_marks(seg))).astype(BF16)
        vf_ref[o, dst, :] = (dot(x, wv_out[:, far_cols]) + ones_lane).astype(BF16)
        return seg

    def near_rows(o, b, ref):
        first, count = ((GROUP - edge, edge), (0, GROUP), (0, edge))[b]
        x = ref[pl.ds(o * GROUP + first, count), :]
        pos = base + (b - 1) * ROWS + DIL * (iota((count, 1), 0) + first) + o
        seg = segment_of(pos, near_ends)
        dst = pl.ds((0, edge, edge + GROUP)[b], count)
        kn_ref[o, dst, :] = (dot(x, wk_out[:, near_cols]) + tiled(key_marks(seg))).astype(BF16)
        vn_ref[o, dst, :] = (dot(x, wv_out[:, near_cols]) + ones_lane[:count]).astype(BF16)
        return seg

    for o in range(DIL):
        rows = pl.ds(o * GROUP, GROUP)
        q_ref[rows, :] = dot(normed_ref[rows, :], wq_out[...]).astype(BF16)
        qm_ref[0, rows, :] = query_marks(near_rows(o, 1, normed_ref)).astype(BF16)
        qm_ref[1, rows, :] = query_marks(far_rows(o, 1, normed_ref)).astype(BF16)
    for c in near_copies:
        c.wait()
    for o in range(DIL):
        near_rows(o, 0, left_ref)
        near_rows(o, 2, right_ref)

    def near_block(b, carry):
        g = pl.multiple_of(b * 32, 32)

        def joined(ref, n, j):
            cols = slice(j * LANES, (j + 1) * LANES)
            return jnp.concatenate([ref[o, pl.ds(g, n), cols] for o in range(DIL)], axis=0)

        def query(j):
            cols = slice(j * LANES, (j + 1) * LANES)
            return jnp.concatenate(
                [q_ref[pl.ds(o * GROUP + g, 32), cols] for o in range(DIL)], axis=0
            )

        marks = jnp.concatenate(
            [qm_ref[0, pl.ds(o * GROUP + g, 32), :] for o in range(DIL)], axis=0
        )
        out = attend(query, marks, lambda j: joined(kn_ref, 160, j), lambda j: joined(vn_ref, 160, j))
        for o in range(DIL):
            ctx_ref[pl.ds(o * GROUP + g, 32), near_cols] = out[o * 32 : (o + 1) * 32, :]
        return carry

    lax.fori_loop(0, ROWS // 128, near_block, 0)
    for c in far_copies:
        c.wait()
    for o in range(DIL):
        far_rows(o, 0, left_ref)
        far_rows(o, 2, right_ref)

    def far_block(i, carry):
        o, half = i // 2, i % 2
        g = pl.multiple_of(half * 128, 128)
        rows = pl.ds(pl.multiple_of(o * GROUP + g, 128), 128)
        ctx_ref[rows, far_cols] = attend(
            lambda j: q_ref[rows, PW + j * LANES : PW + (j + 1) * LANES],
            qm_ref[1, rows, :],
            lambda j: kf_ref[o, pl.ds(g, 640), j * LANES : (j + 1) * LANES],
            lambda j: vf_ref[o, pl.ds(g, 640), j * LANES : (j + 1) * LANES],
        )
        return carry

    lax.fori_loop(0, ROWS // 128, far_block, 0)

    for o in range(DIL):
        rows = pl.ds(o * GROUP, GROUP)
        out = start_ref[rows, :].astype(F32) + dot(ctx_ref[rows, :], wo_out[...])
        s_ref[rows, :] = out.astype(BF16)
    step = 256
    for k in range(ROWS // step):
        r = iota((step, ROWS), 0) + k * step
        pick = jnp.where(
            iota((step, ROWS), 1) == (r % DIL) * GROUP + r // DIL, 1.0, 0.0
        ).astype(BF16)
        normed_ref[pl.ds(k * step, step), :] = dot(pick, s_ref[...]).astype(BF16)
    sel = jnp.where(
        iota((8, ROWS), 0) == iota((8, ROWS), 1) // REGION, tissue_ref[...], 0
    )
    pooled = dot(sel.astype(F32).astype(BF16), normed_ref[...]) / REGION
    store = pltpu.make_async_copy(normed_ref, feat_hbm, load_sem.at[7])
    store.start()

    core = reg % 2
    at = {"z": enc, "x": (reg // 2) % 4, "y": reg // 8}

    def device(shift):
        c = {a: (at[a] + shift.get(a, 0)) % 4 for a in AXES}
        return (c["z"], (c["y"] * 4 + c["x"]) * 2 + (core + shift.get("core", 0)) % 2)

    center = pooled - jnp.mean(pooled, axis=1, keepdims=True)
    var = jnp.mean(center * center, axis=1, keepdims=True)
    norm = center * lax.rsqrt(var + EPS)
    row = iota((8, D), 0)
    norm = jnp.where(row < 4, norm, 0.0)
    swapped = jnp.concatenate([norm[4:], norm[:4]], axis=0)
    pair_ref[0] = jnp.where(core == 0, norm, swapped)
    first = pltpu.make_async_remote_copy(
        src_ref=pair_ref.at[0], dst_ref=pair_ref.at[1], send_sem=ps, recv_sem=pr,
        device_id=device({"core": 1}), device_id_type=MESH,
    )
    first.start()
    first.wait()
    chip = pair_ref[0] + pair_ref[1]
    mine = jnp.where(core == 0, chip[:, :HALF], chip[:, HALF:])
    orders = [("z", "y", "x"), ("y", "x", "z"), ("x", "z", "y")]

    def offset(order):
        return ((at[order[2]] * 4 + at[order[1]]) * 4 + at[order[0]]) * 8

    for t, order in enumerate(orders):
        start = pl.multiple_of(offset(order), 8)
        half_ref[t, pl.ds(start, 8), :] = mine[:, t * LANES : (t + 1) * LANES]
    size = 8
    for stage in range(3):
        copies = []
        for t, order in enumerate(orders):
            start = pl.multiple_of(offset(order) // size * size, size)
            for k in (1, 2, 3):
                window = half_ref.at[t, pl.ds(start, size), :]
                copies.append(
                    pltpu.make_async_remote_copy(
                        src_ref=window, dst_ref=window,
                        send_sem=ss.at[stage, t, k - 1], recv_sem=rs.at[stage, t, k - 1],
                        device_id=device({order[stage]: k}), device_id_type=MESH,
                    )
                )
        for c in copies:
            c.start()
        for c in copies:
            c.wait()
        size *= 4
    last = pltpu.make_async_remote_copy(
        src_ref=half_ref, dst_ref=full_ref, send_sem=cs, recv_sem=cr,
        device_id=device({"core": 1}), device_id_type=MESH,
    )
    last.start()
    last.wait()

    for x in range(4):
        for y in range(4):
            for z in range(4):
                i = {"x": x, "y": y, "z": z}
                to = pl.ds(((x * 4 + y) * 4 + z) * 8, 8)
                for t, order in enumerate(orders):
                    src = pl.ds(((i[order[2]] * 4 + i[order[1]]) * 4 + i[order[0]]) * 8, 8)
                    a, b = half_ref[t, src, :], full_ref[t, src, :]
                    np_ref[to, t * LANES : (t + 1) * LANES] = jnp.where(core == 0, a, b)
                    np_ref[to, HALF + t * LANES : HALF + (t + 1) * LANES] = jnp.where(core == 0, b, a)

    n = PEERS * 4
    hp = lax.Precision.HIGHEST
    hosp = hosp_ref[...]
    ones = jnp.sum(hosp).astype(F32)
    per_slide = float(n // NENC)
    count_one = ones * per_slide
    count_zero = (NENC - ones) * per_slide

    def weights(slide, axis):
        label = jnp.zeros(slide.shape, I32)
        for s in range(NENC):
            label = jnp.where(slide == s, hosp[:, s : s + 1], label)
        return jnp.where(label == 1, 1.0 / count_one, -1.0 / count_zero)

    w_col = weights((iota((n, 1), 0) // 8) % 4, 0)
    w_row = weights((iota((1, n), 1) // 8) % 4, 1)
    normal = np_ref[...]
    emb = dot3(normal, wkern_ref[...])
    sq = emb * emb
    sq_col = jnp.sum(sq, axis=1, keepdims=True)
    sq_row = lax.dot_general(
        jnp.ones((8, sq.shape[1]), F32), sq, (((1,), (1,)), ((), ())), precision=hp,
        preferred_element_type=F32,
    )[0:1, :]
    inner = dot3(emb, emb, 1, 1)
    kern = jnp.exp(-(sq_col + sq_row - 2.0 * inner) / (2.0 * emb.shape[1])) * w_row
    sums = jnp.sum(kern, axis=1, keepdims=True)
    moments = dot3(kern, emb)
    stat = n * jnp.sum(w_col * sums)
    stat_ref[0, 0] = stat
    g = (-2.0 * n / emb.shape[1]) * w_col * (sums * emb - moments)
    grad_ref[...] = 100.0 * dot3(normal, g, 0, 0)
    store.wait()


def local(
    embeddings, tile_position, w_in, ln_gain, w_query, w_key, w_value, w_out,
    near_lengths, far_lengths, tissue, hospital, w_kernel,
):
    sds = jax.ShapeDtypeStruct
    dma, vmem = pltpu.SemaphoreType.DMA, pltpu.VMEM
    rows = vmem((ROWS, D), BF16)
    square = vmem((D, D), BF16)
    padded = vmem((D, PAIRS * LANES), BF16)
    features, stat, grad = pl.pallas_call(
        slide_kernel,
        out_shape=(sds((ROWS, D), BF16), sds((1, 1), F32), sds((D, 256), F32)),
        in_specs=[ANY, VM, ANY, VM, ANY, ANY, ANY, ANY, VM, VM, VM, VM, ANY],
        out_specs=(ANY, pl.BlockSpec(memory_space=pltpu.SMEM), VM),
        scratch_shapes=[
            vmem((ROWS, DIN), BF16), vmem((DIN, D), BF16), square, square, square, square,
            vmem((D, 256), F32), padded, padded, padded, vmem((PAIRS * LANES, D), BF16),
            rows, rows, rows,
            vmem((PEERS, LANES), F32),
            vmem((2 * ROWS, HALF), BF16), vmem((PEERS, 1, LANES), F32),
            vmem((2 * ROWS, HALF), BF16), vmem((PEERS, 1, LANES), F32),
            rows, rows,
            vmem((ROWS, 2 * PW), BF16), vmem((2, ROWS, LANES), BF16),
            vmem((DIL, GROUP + 128, PW), BF16), vmem((DIL, GROUP + 128, PW), BF16),
            vmem((DIL, 3 * GROUP, PW), BF16), vmem((DIL, 3 * GROUP, PW), BF16),
            vmem((ROWS, 2 * PW), BF16),
            vmem((2, 8, D), F32), vmem((3, 512, LANES), F32), vmem((3, 512, LANES), F32),
            vmem((512, D), F32),
            dma((8,)), dma, dma, dma, dma, dma((2,)), dma((2, 2, DIL)), dma((2, 2, DIL)),
            dma, dma, dma((3, 3, 3)), dma((3, 3, 3)), dma, dma,
        ],
        compiler_params=params(collective_id=0, has_side_effects=True),
        name="slide",
    )(
        embeddings, tile_position.reshape(1, ROWS), w_in, ln_gain, w_query, w_key, w_value, w_out,
        near_lengths, far_lengths, tissue.reshape(1, ROWS), hospital.reshape(1, NENC), w_kernel,
    )
    return features, stat.reshape(()), grad


def solution(mesh):
    split = P(("enc", "region"))
    return jax.shard_map(
        local,
        mesh=mesh,
        in_specs=(
            P(("enc", "region"), None), split, P(), P(), P(), P(), P(), P(), P(), P(), split, P(), P(),
        ),
        out_specs=(P(("enc", "region"), None), P(), P()),
        check_vma=False,
    )
```

time: 125 us -> 106 us (0.85)
  Pallas kernels: 118 us -> 99.5 us
  local copies, waits for them, and re-layouts: 6.06 us -> 3.61 us
  between operations: 0.66 us -> 2.48 us
    pallas_call x3 -> x1, Pallas kernels: 118 us -> 99.5 us  [local(): pl.pallas_call(slide_kernel, out_shape=(sds((ROWS, D), BF16), sds((1, 1),...]
    reshape x1 -> x0, local copies, waits for them, and re-layouts: 1.26 us -> none  [local(): ln_gain.reshape(1, D)]
where the time goes in v3:
time: 106 us
  Pallas kernels  99.5 us (94%)
  local copies, waits for them, and re-layouts  3.61 us (3%)
  between operations  2.48 us (2%)
    pallas_call x1, Pallas kernels, local(): pl.pallas_call(slide_kernel, out_shape=(sds((ROWS, D), BF16), sds((1, 1),...  99.5 us
    unnamed x4, local copies, waits for them, and re-layouts  3.61 us

profile of v3, /device:TPU:1, one launch (start us, length us, event | category | flops | bytes accessed | tf_op | source)
XLA Modules:
  0.0 105.6 jit_solution(8780480087747362608)
XLA Ops:
  0.6 99.5 %slide.1 = (bf16[1024,768]{1,0:T(8,128)(2,1)}, f32[1,1]{1,0:T(1,128)}, f32[768,256]{1,0:T(8,128)}) custom-call(bf16[1024,1536]{1,0:T(8,128)(2,1)} %emb_hbm.1, s32[1,1024]{1,0:T(1,128)} %bitcast.4, bf16[1536,768]{1,0:T(8,128)(2,1)} %win_hbm.1, bf16[768]{0:T(1024)(128)(2,1)} %gain_ref.1, bf16[768,768]{1,0:T(8,128)(2,1)} %wq_hbm.1, bf16[768,768]{1,0:T(8,128)(2,1)} %wk_hbm.1, ...), custom_call_target="tpu_custom_call" | custom-call | tf_op jit(solution)/shard_map/slide/pallas_call | solution.py:499
  100.2 0.0 copy-start
  100.2 2.7 %copy.19 = bf16[1024,768]{1,0:T(8,128)(2,1)} copy(bf16[1024,768]{1,0:T(8,128)(2,1)} %get-tuple-element.12) | data formatting | bytes 3145728
  103.6 0.0 copy-done
  103.6 0.9 copy.21
Async XLA Ops:
  100.2 3.4 %copy-start = (f32[768,256]{1,0:T(8,128)S(1)}, f32[768,256]{1,0:T(8,128)}, u32[]{:S(2)}) copy-start(f32[768,256]{1,0:T(8,128)} %get-tuple-element.14) | copy-start | bytes 2359300

commit v4 on v3

--- a/solution.py
+++ b/solution.py
@@ -26,6 +26,7 @@
 NREGION = 32
 PEERS = NENC * NREGION
 CAP = 8
+SEND_UNROLL = 1
 SPREAD = 45
 HALF = D // 2
 EPS = 1e-05
@@ -131,20 +132,24 @@
     start_ref, normed_ref, s_ref, tab_ref, xs_ref, ps_ref, xr_ref, pr_ref,
     left_ref, right_ref, q_ref, qm_ref, kn_ref, vn_ref, kf_ref, vf_ref, ctx_ref,
     pair_ref, half_ref, full_ref, np_ref,
-    load_sem, sx, rx, sp, rp, own, send_sem, recv_sem, ps, pr, ss, rs, cs, cr,
+    load_sem, sx, rx, sp, rp, own, send_sem, recv_sem, pair_send, pair_recv, ss, rs, entered,
 ):
-    me = lax.axis_index("enc") * NREGION + lax.axis_index("region")
+    enc, reg = lax.axis_index("enc"), lax.axis_index("region")
+    me = enc * NREGION + reg
+    core = reg % 2
+    at = {"z": enc, "x": (reg // 2) % 4, "y": reg // 8}
+
+    def device(shift):
+        c = {a: (at[a] + shift.get(a, 0)) % 4 for a in AXES}
+        return (c["z"], (c["y"] * 4 + c["x"]) * 2 + (core + shift.get("core", 0)) % 2)
+
     chunk = 2 * CAP
     barrier = pltpu.get_barrier_semaphore()
 
-    def signal(k, carry):
-        peer = (me + k) % PEERS
-        pl.semaphore_signal(
-            barrier, inc=1, device_id=(peer // NREGION, peer % NREGION), device_id_type=MESH
-        )
-        return carry
-
-    lax.fori_loop(1, PEERS, signal, 0)
+    plane_yz = [{"z": i, "y": j} for i in range(4) for j in range(4) if i or j]
+    line_x = [{"x": i, "core": c} for i in range(4) for c in range(2) if i or c]
+    for shift in plane_yz + line_x:
+        pl.semaphore_signal(barrier, inc=1, device_id=device(shift), device_id_type=MESH)
     loads = [
         pltpu.make_async_copy(src, dst, load_sem.at[i])
         for i, (src, dst) in enumerate(
@@ -187,6 +192,9 @@
         s_ref[pl.ds(k * step, step), :] = dot(
             emb_ref[pl.ds(k * step, step), :], w_ref[...]
         ).astype(BF16)
+    pl.semaphore_wait(barrier, len(plane_yz + line_x))
+    for shift in line_x:
+        pl.semaphore_signal(entered, inc=1, device_id=device(shift), device_id_type=MESH)
     for k in range(ROWS // step):
         pick = jnp.where(iota((step, ROWS), 0) + k * step == rank, 1.0, 0.0).astype(BF16)
         moved = dot(pick, s_ref[...]).reshape(step // CAP, CAP, D)
@@ -199,23 +207,22 @@
     mine_p = pltpu.make_async_copy(ps_ref.at[me], pr_ref.at[me], own.at[1])
     mine_x.start()
     mine_p.start()
-    pl.semaphore_wait(barrier, PEERS - 1)
+    pl.semaphore_wait(entered, len(line_x))
 
     def send(k, carry):
         peer = (me + k * SPREAD) % PEERS
-        where = (peer // NREGION, peer % NREGION)
         pltpu.make_async_remote_copy(
             src_ref=ps_ref.at[peer], dst_ref=pr_ref.at[me],
-            send_sem=sp, recv_sem=rp, device_id=where, device_id_type=MESH,
+            send_sem=sp, recv_sem=rp, device_id=peer, device_id_type=pl.DeviceIdType.LOGICAL,
         ).start()
         pltpu.make_async_remote_copy(
             src_ref=xs_ref.at[pl.ds(peer * chunk, chunk), :],
             dst_ref=xr_ref.at[pl.ds(me * chunk, chunk), :],
-            send_sem=sx, recv_sem=rx, device_id=where, device_id_type=MESH,
+            send_sem=sx, recv_sem=rx, device_id=peer, device_id_type=pl.DeviceIdType.LOGICAL,
         ).start()
         return carry
 
-    lax.fori_loop(1, PEERS, send, 0)
+    lax.fori_loop(1, PEERS, send, 0, unroll=SEND_UNROLL)
 
     for c in loads[2:]:
         c.wait()
@@ -266,7 +273,6 @@
         var = jnp.mean(center * center, axis=1, keepdims=True)
         normed_ref[pl.ds(k * step, step), :] = (center * lax.rsqrt(var + EPS) * gain).astype(BF16)
 
-    enc, reg = lax.axis_index("enc"), lax.axis_index("region")
     after, before = (reg + 1) % NREGION, (reg + NREGION - 1) % NREGION
     edge = GROUP // 4
     near_copies, far_copies = [], []
@@ -385,13 +391,6 @@
     store = pltpu.make_async_copy(normed_ref, feat_hbm, load_sem.at[7])
     store.start()
 
-    core = reg % 2
-    at = {"z": enc, "x": (reg // 2) % 4, "y": reg // 8}
-
-    def device(shift):
-        c = {a: (at[a] + shift.get(a, 0)) % 4 for a in AXES}
-        return (c["z"], (c["y"] * 4 + c["x"]) * 2 + (core + shift.get("core", 0)) % 2)
-
     center = pooled - jnp.mean(pooled, axis=1, keepdims=True)
     var = jnp.mean(center * center, axis=1, keepdims=True)
     norm = center * lax.rsqrt(var + EPS)
@@ -400,7 +399,7 @@
     swapped = jnp.concatenate([norm[4:], norm[:4]], axis=0)
     pair_ref[0] = jnp.where(core == 0, norm, swapped)
     first = pltpu.make_async_remote_copy(
-        src_ref=pair_ref.at[0], dst_ref=pair_ref.at[1], send_sem=ps, recv_sem=pr,
+        src_ref=pair_ref.at[0], dst_ref=pair_ref.at[1], send_sem=pair_send, recv_sem=pair_recv,
         device_id=device({"core": 1}), device_id_type=MESH,
     )
     first.start()
@@ -415,31 +414,43 @@
     for t, order in enumerate(orders):
         start = pl.multiple_of(offset(order), 8)
         half_ref[t, pl.ds(start, 8), :] = mine[:, t * LANES : (t + 1) * LANES]
-    size = 8
-    for stage in range(3):
-        copies = []
-        for t, order in enumerate(orders):
-            start = pl.multiple_of(offset(order) // size * size, size)
-            for k in (1, 2, 3):
-                window = half_ref.at[t, pl.ds(start, size), :]
-                copies.append(
-                    pltpu.make_async_remote_copy(
-                        src_ref=window, dst_ref=window,
-                        send_sem=ss.at[stage, t, k - 1], recv_sem=rs.at[stage, t, k - 1],
-                        device_id=device({order[stage]: k}), device_id_type=MESH,
-                    )
-                )
+    def plane(order):
+        return [{order[0]: a, order[1]: b} for a in range(4) for b in range(4) if a or b]
+
+    def remote(window, sems, peer):
+        return pltpu.make_async_remote_copy(
+            src_ref=window, dst_ref=window, send_sem=ss.at[sems], recv_sem=rs.at[sems],
+            device_id=device(peer), device_id_type=MESH,
+        )
+
+    first, second, third = [], [], []
+    for t, order in enumerate(orders):
+        start = pl.multiple_of(offset(order), 8)
+        window = half_ref.at[t, pl.ds(start, 8), :]
+        first.append([remote(window, (t, i), p) for i, p in enumerate(plane(order))])
+        window = half_ref.at[t, pl.ds(pl.multiple_of(start // 128 * 128, 128), 128), :]
+        second.append([remote(window, (t, 15 + k), {order[2]: k + 1}) for k in range(3)])
+        third.append(
+            pltpu.make_async_remote_copy(
+                src_ref=half_ref.at[t], dst_ref=full_ref.at[t],
+                send_sem=ss.at[t, 18], recv_sem=rs.at[t, 18],
+                device_id=device({"core": 1}), device_id_type=MESH,
+            )
+        )
+    for copies in first:
         for c in copies:
             c.start()
-        for c in copies:
+    for t in range(3):
+        for c in first[t]:
             c.wait()
-        size *= 4
-    last = pltpu.make_async_remote_copy(
-        src_ref=half_ref, dst_ref=full_ref, send_sem=cs, recv_sem=cr,
-        device_id=device({"core": 1}), device_id_type=MESH,
-    )
-    last.start()
-    last.wait()
+        for c in second[t]:
+            c.start()
+    for t in range(3):
+        for c in second[t]:
+            c.wait()
+        third[t].start()
+    for t in range(3):
+        third[t].wait()
 
     for x in range(4):
         for y in range(4):
@@ -516,7 +527,7 @@
             vmem((2, 8, D), F32), vmem((3, 512, LANES), F32), vmem((3, 512, LANES), F32),
             vmem((512, D), F32),
             dma((8,)), dma, dma, dma, dma, dma((2,)), dma((2, 2, DIL)), dma((2, 2, DIL)),
-            dma, dma, dma((3, 3, 3)), dma((3, 3, 3)), dma, dma,
+            dma, dma, dma((3, 19)), dma((3, 19)), pltpu.SemaphoreType.REGULAR,
         ],
         compiler_params=params(collective_id=0, has_side_effects=True),
         name="slide",

time: 106 us -> 102 us (0.962)
  Pallas kernels: 99.5 us -> 95.3 us
    pallas_call x1, Pallas kernels: 99.5 us -> 95.3 us  [local(): pl.pallas_call(slide_kernel, out_shape=(sds((ROWS, D), BF16), sds((1, 1),...]
where the time goes in v4:
time: 102 us; the launch traced here: 101 us
  Pallas kernels  95.3 us (93%)
  local copies, waits for them, and re-layouts  3.61 us (4%)
  between operations  2.48 us (2%)
    pallas_call x1, Pallas kernels, local(): pl.pallas_call(slide_kernel, out_shape=(sds((ROWS, D), BF16), sds((1, 1),...  95.3 us
    unnamed x4, local copies, waits for them, and re-layouts  3.61 us

profile of v4, /device:TPU:1, one launch (start us, length us, event | category | flops | bytes accessed | tf_op | source)
XLA Modules:
  0.0 101.4 jit_solution(558819777141042405)
XLA Ops:
  0.6 95.3 %slide.1 = (bf16[1024,768]{1,0:T(8,128)(2,1)}, f32[1,1]{1,0:T(1,128)}, f32[768,256]{1,0:T(8,128)}) custom-call(bf16[1024,1536]{1,0:T(8,128)(2,1)} %emb_hbm.1, s32[1,1024]{1,0:T(1,128)} %bitcast.4, bf16[1536,768]{1,0:T(8,128)(2,1)} %win_hbm.1, bf16[768]{0:T(1024)(128)(2,1)} %gain_ref.1, bf16[768,768]{1,0:T(8,128)(2,1)} %wq_hbm.1, bf16[768,768]{1,0:T(8,128)(2,1)} %wk_hbm.1, ...), custom_call_target="tpu_custom_call" | custom-call | tf_op jit(solution)/shard_map/slide/pallas_call | solution.py:510
  95.9 0.0 copy-start
  95.9 2.7 %copy.19 = bf16[1024,768]{1,0:T(8,128)(2,1)} copy(bf16[1024,768]{1,0:T(8,128)(2,1)} %get-tuple-element.12) | data formatting | bytes 3145728
  99.3 0.0 copy-done
  99.4 0.9 copy.21
Async XLA Ops:
  95.9 3.4 %copy-start = (f32[768,256]{1,0:T(8,128)S(1)}, f32[768,256]{1,0:T(8,128)}, u32[]{:S(2)}) copy-start(f32[768,256]{1,0:T(8,128)} %get-tuple-element.14) | copy-start | bytes 2359300

commit v5 on v4

--- a/solution.py
+++ b/solution.py
@@ -130,7 +130,7 @@
     feat_hbm, stat_ref, grad_ref,
     emb_ref, w_ref, wq_ref, wk_ref, wv_ref, wo_ref, wkern_ref, wq_out, wk_out, wv_out, wo_out,
     start_ref, normed_ref, s_ref, tab_ref, xs_ref, ps_ref, xr_ref, pr_ref,
-    left_ref, right_ref, q_ref, qm_ref, kn_ref, vn_ref, kf_ref, vf_ref, ctx_ref,
+    sel_ref, left_ref, right_ref, q_ref, qm_ref, kn_ref, vn_ref, kf_ref, vf_ref, ctx_ref,
     pair_ref, half_ref, full_ref, np_ref,
     load_sem, sx, rx, sp, rp, own, send_sem, recv_sem, pair_send, pair_recv, ss, rs, entered,
 ):
@@ -234,6 +234,13 @@
     for j in range(PAIRS):
         wo_out[pl.ds(LANES * j, 2 * HEAD), :] = wo_ref[pl.ds(2 * HEAD * j, 2 * HEAD), :]
         wo_out[pl.ds(LANES * j + 2 * HEAD, LANES - 2 * HEAD), :] = jnp.zeros((LANES - 2 * HEAD, D), BF16)
+
+    chosen = jnp.where(
+        iota((8, ROWS), 0) == iota((8, ROWS), 1) // REGION, tissue_ref[...], 0
+    ).astype(F32).astype(BF16)
+    for o in range(DIL):
+        moves = iota((ROWS, GROUP), 0) == iota((ROWS, GROUP), 1) * DIL + o
+        sel_ref[:, o * GROUP : (o + 1) * GROUP] = dot(chosen, jnp.where(moves, 1.0, 0.0).astype(BF16))
 
     mine_x.wait()
     mine_p.wait()
@@ -377,19 +384,14 @@
         rows = pl.ds(o * GROUP, GROUP)
         out = start_ref[rows, :].astype(F32) + dot(ctx_ref[rows, :], wo_out[...])
         s_ref[rows, :] = out.astype(BF16)
-    step = 256
-    for k in range(ROWS // step):
+    pooled = dot(sel_ref[...].astype(BF16), s_ref[...]) / REGION
+
+    def reorder(k):
         r = iota((step, ROWS), 0) + k * step
         pick = jnp.where(
             iota((step, ROWS), 1) == (r % DIL) * GROUP + r // DIL, 1.0, 0.0
         ).astype(BF16)
         normed_ref[pl.ds(k * step, step), :] = dot(pick, s_ref[...]).astype(BF16)
-    sel = jnp.where(
-        iota((8, ROWS), 0) == iota((8, ROWS), 1) // REGION, tissue_ref[...], 0
-    )
-    pooled = dot(sel.astype(F32).astype(BF16), normed_ref[...]) / REGION
-    store = pltpu.make_async_copy(normed_ref, feat_hbm, load_sem.at[7])
-    store.start()
 
     center = pooled - jnp.mean(pooled, axis=1, keepdims=True)
     var = jnp.mean(center * center, axis=1, keepdims=True)
@@ -403,6 +405,7 @@
         device_id=device({"core": 1}), device_id_type=MESH,
     )
     first.start()
+    reorder(0)
     first.wait()
     chip = pair_ref[0] + pair_ref[1]
     mine = jnp.where(core == 0, chip[:, :HALF], chip[:, HALF:])
@@ -440,6 +443,10 @@
     for copies in first:
         for c in copies:
             c.start()
+    for k in range(1, ROWS // step):
+        reorder(k)
+    store = pltpu.make_async_copy(normed_ref, feat_hbm, load_sem.at[7])
+    store.start()
     for t in range(3):
         for c in first[t]:
             c.wait()
@@ -519,7 +526,7 @@
             vmem((PEERS, LANES), F32),
             vmem((2 * ROWS, HALF), BF16), vmem((PEERS, 1, LANES), F32),
             vmem((2 * ROWS, HALF), BF16), vmem((PEERS, 1, LANES), F32),
-            rows, rows,
+            vmem((8, ROWS), F32), rows, rows,
             vmem((ROWS, 2 * PW), BF16), vmem((2, ROWS, LANES), BF16),
             vmem((DIL, GROUP + 128, PW), BF16), vmem((DIL, GROUP + 128, PW), BF16),
             vmem((DIL, 3 * GROUP, PW), BF16), vmem((DIL, 3 * GROUP, PW), BF16),

time: 102 us -> 99.9 us (0.979)
  Pallas kernels: 95.3 us -> 93.6 us
    pallas_call x1, Pallas kernels: 95.3 us -> 93.6 us  [local(): pl.pallas_call(slide_kernel, out_shape=(sds((ROWS, D), BF16), sds((1, 1),...]
where the time goes in v5:
time: 99.9 us; the launch traced here: 99.7 us
  Pallas kernels  93.6 us (94%)
  local copies, waits for them, and re-layouts  3.61 us (4%)
  between operations  2.48 us (2%)
    pallas_call x1, Pallas kernels, local(): pl.pallas_call(slide_kernel, out_shape=(sds((ROWS, D), BF16), sds((1, 1),...  93.6 us
    unnamed x4, local copies, waits for them, and re-layouts  3.61 us

profile of v5, /device:TPU:1, one launch (start us, length us, event | category | flops | bytes accessed | tf_op | source)
XLA Modules:
  0.0 99.7 jit_solution(10074964655712978238)
XLA Ops:
  0.6 93.6 %slide.1 = (bf16[1024,768]{1,0:T(8,128)(2,1)}, f32[1,1]{1,0:T(1,128)}, f32[768,256]{1,0:T(8,128)}) custom-call(bf16[1024,1536]{1,0:T(8,128)(2,1)} %emb_hbm.1, s32[1,1024]{1,0:T(1,128)} %bitcast.4, bf16[1536,768]{1,0:T(8,128)(2,1)} %win_hbm.1, bf16[768]{0:T(1024)(128)(2,1)} %gain_ref.1, bf16[768,768]{1,0:T(8,128)(2,1)} %wq_hbm.1, bf16[768,768]{1,0:T(8,128)(2,1)} %wk_hbm.1, ...), custom_call_target="tpu_custom_call" | custom-call | tf_op jit(solution)/shard_map/slide/pallas_call | solution.py:517
  94.3 0.0 copy-start
  94.3 2.7 %copy.19 = bf16[1024,768]{1,0:T(8,128)(2,1)} copy(bf16[1024,768]{1,0:T(8,128)(2,1)} %get-tuple-element.12) | data formatting | bytes 3145728
  97.7 0.0 copy-done
  97.7 0.9 copy.21
Async XLA Ops:
  94.3 3.4 %copy-start = (f32[768,256]{1,0:T(8,128)S(1)}, f32[768,256]{1,0:T(8,128)}, u32[]{:S(2)}) copy-start(f32[768,256]{1,0:T(8,128)} %get-tuple-element.14) | copy-start | bytes 2359300

commit v6 on v5

--- a/solution.py
+++ b/solution.py
@@ -360,9 +360,9 @@
         return carry
 
     lax.fori_loop(0, ROWS // 128, near_block, 0)
-    for c in far_copies:
-        c.wait()
     for o in range(DIL):
+        for c in far_copies[2 * o : 2 * o + 2]:
+            c.wait()
         far_rows(o, 0, left_ref)
         far_rows(o, 2, right_ref)
 

time: 99.9 us -> 99.6 us (level)
  no operation moved by 1% of the time
where the time goes in v6:
time: 99.6 us; the launch traced here: 99.5 us
  Pallas kernels  93.4 us (94%)
  local copies, waits for them, and re-layouts  3.61 us (4%)
  between operations  2.48 us (2%)
    pallas_call x1, Pallas kernels, local(): pl.pallas_call(slide_kernel, out_shape=(sds((ROWS, D), BF16), sds((1, 1),...  93.4 us
    unnamed x4, local copies, waits for them, and re-layouts  3.61 us

profile of v6, /device:TPU:1, one launch (start us, length us, event | category | flops | bytes accessed | tf_op | source)
XLA Modules:
  0.0 99.5 jit_solution(13327158486887139756)
XLA Ops:
  0.6 93.4 %slide.1 = (bf16[1024,768]{1,0:T(8,128)(2,1)}, f32[1,1]{1,0:T(1,128)}, f32[768,256]{1,0:T(8,128)}) custom-call(bf16[1024,1536]{1,0:T(8,128)(2,1)} %emb_hbm.1, s32[1,1024]{1,0:T(1,128)} %bitcast.4, bf16[1536,768]{1,0:T(8,128)(2,1)} %win_hbm.1, bf16[768]{0:T(1024)(128)(2,1)} %gain_ref.1, bf16[768,768]{1,0:T(8,128)(2,1)} %wq_hbm.1, bf16[768,768]{1,0:T(8,128)(2,1)} %wk_hbm.1, ...), custom_call_target="tpu_custom_call" | custom-call | tf_op jit(solution)/shard_map/slide/pallas_call | solution.py:517
  94.0 0.0 copy-start
  94.0 2.7 %copy.19 = bf16[1024,768]{1,0:T(8,128)(2,1)} copy(bf16[1024,768]{1,0:T(8,128)(2,1)} %get-tuple-element.12) | data formatting | bytes 3145728
  97.4 0.0 copy-done
  97.4 0.9 copy.21
Async XLA Ops:
  94.0 3.4 %copy-start = (f32[768,256]{1,0:T(8,128)S(1)}, f32[768,256]{1,0:T(8,128)}, u32[]{:S(2)}) copy-start(f32[768,256]{1,0:T(8,128)} %get-tuple-element.14) | copy-start | bytes 2359300
